TPU v7x, 32 devices: a whole 2x2x4 slice. The times are simulated.
32 devices in a mesh: groups: 2 (over x), strip: 16 (over z, y, core).
Axes of the slice: x: 2, y: 2, z: 4, core: 2. Of those that a mesh axis runs over, the one named last changes fastest.
Arguments:
- incoming_wave: float32 [8, 2, 256, 1024], P('groups', None, 'strip'), parts along dimension 0, may hold values from -64 to 64
- speed_class_map: int32 [4, 256, 1024], P('groups', 'strip'), parts along dimension 0, may hold values from 0 to 15
- spectral_entry_index: int32 [8, 4], P('groups'), parts along dimension 0, may hold values from 0 to 15
- filter_weights: float32 [16, 16, 2, 13], replicated, may hold values from -1.6 to 1.6
- scaled_pulsations: float32 [16], replicated, may hold values from 1 to 6
- inverse_speed_classes: float32 [16], replicated, may hold values from 0.3 to 1.5
Outputs:
- image: float32 [4, 256, 1024], P('groups', 'strip'), parts along dimension 0
- handed: float32 [8, 2, 256, 1024], P('groups', None, 'strip'), parts along dimension 0
There are 2 independent parts, one for each index of `groups`. A program takes and returns all parts, laid end to end along the dimension named above; an argument that names none is the same for every part. Nothing has to cross between parts.
All inputs are finite; a program needn't handle non-finite values.
Results may differ from a plain program's by a relative error of at most 0.0003.
Values sent between devices are 32-bit elements; how exact they have to be, the bound alone decides.
No kernel may reach another device: no remote copies, remote signals or barrier semaphores. Data moves between devices by JAX's collectives and lax.ppermute only.
A program may use at most 128 MiB of HBM per device.

v0:
```python
import functools

import jax
import jax.numpy as jnp
from jax import lax
from jax.experimental import pallas as pl
from jax.experimental.pallas import tpu as pltpu
from jax.sharding import PartitionSpec as P

SECTIONS = 4
LEVELS = 2
ORDER = 12
NFREQ = 4
NBIN = 16
NW = 16


def extended_2(shard, sides, width):
    for axis, dim in sides:
        devices, length = (lax.axis_size(axis), shard.shape[dim])
        up = [(i, (i + 1) % devices) for i in range(devices)]
        down = [(j, i) for i, j in up]
        last = lax.slice_in_dim(shard, length - width, length, axis=dim)
        initial = lax.slice_in_dim(shard, 0, width, axis=dim)
        before = lax.ppermute(last, axis, up)
        after = lax.ppermute(initial, axis, down)
        shard = jnp.concatenate([before, shard, after], axis=dim)
    return shard


def from_behind(shard, axis, by):
    devices = lax.axis_size(axis)
    return lax.ppermute(shard, axis, [(i, (i + by) % devices) for i in range(devices)])


def stencil_padded(padded):
    vertical = padded[:, :, :-2, :] + padded[:, :, 2:, :]
    middle = padded[:, :, 1:-1, :]
    return (
        -0.5 * middle[..., 1:-1]
        + 0.25 * (vertical[..., 1:-1] + middle[..., :-2] + middle[..., 2:])
        + 0.125 * (vertical[..., :-2] + vertical[..., 2:])
    )


def complex_times(coeff, field):
    real_part = coeff[:, 0] * field[:, 0] - coeff[:, 1] * field[:, 1]
    imag_part = coeff[:, 0] * field[:, 1] + coeff[:, 1] * field[:, 0]
    return jnp.stack([real_part, imag_part], axis=1)


def strip_shards(
    incoming_wave,
    speed_class_map,
    spectral_entry_index,
    filter_weights,
    scaled_pulsations,
    inverse_speed_classes,
):
    highest = lax.Precision.HIGHEST
    summed_along = incoming_wave.shape[2]
    summed_across = incoming_wave.shape[3]
    strip_count = lax.axis_size("strip")
    lateral_count = strip_count // SECTIONS
    position = (lax.axis_index("strip") - lateral_count // 2) % strip_count
    vertical_slab = position // lateral_count
    lateral_place = position % lateral_count
    section_rows = summed_along * lateral_count
    section_cells = section_rows * summed_across
    margin = ORDER
    extended_rows = summed_along + 2 * margin
    lateral_rows = (
        lateral_place * summed_along - margin + jnp.arange(extended_rows, dtype=jnp.int32)
    )
    inside = ((lateral_rows >= 0) & (lateral_rows < section_rows)).astype(jnp.float32)[
        None, None, :, None
    ]

    def mcclellan_step(field):
        padded = jnp.pad(field, ((0, 0), (0, 0), (1, 1), (0, 0)))
        padded = jnp.pad(padded, ((0, 0), (0, 0), (0, 0), (1, 1)))
        result = stencil_padded(padded)
        result = result * inside
        return result

    def interior(field):
        return field[:, :, margin : margin + summed_along, :]

    def image_downward(field, batch_index):
        freq_row = lax.dynamic_index_in_dim(spectral_entry_index, batch_index, 0, keepdims=False)
        freq_select = (freq_row[:, None] == jnp.arange(NW, dtype=jnp.int32)[None, :]).astype(
            jnp.float32
        )
        freq_coeffs = jnp.einsum("fw,wbck->fbck", freq_select, filter_weights, precision=highest)
        freq_omega = jnp.dot(freq_select, scaled_pulsations, precision=highest)
        wavefield = field
        raws = []
        for level in range(LEVELS):
            cells = speed_class_map[level].reshape(-1)
            bin_onehot = (cells[None, :] == jnp.arange(NBIN, dtype=jnp.int32)[:, None]).astype(
                jnp.float32
            )
            cell_slowness = jnp.dot(inverse_speed_classes, bin_onehot, precision=highest).reshape(
                summed_along, summed_across
            )
            table = jnp.einsum("fbck,bn->kfcn", freq_coeffs, bin_onehot, precision=highest).reshape(
                ORDER + 1, NFREQ, 2, summed_along, summed_across
            )
            extended = extended_2(wavefield, (("strip", 2),), ORDER) * inside
            previous = extended
            current = mcclellan_step(extended)
            accumulated = complex_times(table[0], interior(previous)) + complex_times(
                table[1], interior(current)
            )

            def recursion_step(order_index, state_tuple):
                before, present, running = state_tuple
                following = 2.0 * mcclellan_step(present) - before
                coeff = lax.dynamic_index_in_dim(table, order_index, 0, keepdims=False)
                running = running + complex_times(coeff, interior(following))
                return (present, following, running)

            previous, current, accumulated = lax.fori_loop(
                2, ORDER + 1, recursion_step, (previous, current, accumulated)
            )
            phase_angle = freq_omega[:, None, None] * cell_slowness[None]
            cosine = jnp.cos(phase_angle)
            sine_part = jnp.sin(phase_angle)
            real_part = accumulated[:, 0] * cosine - accumulated[:, 1] * sine_part
            imag_part = accumulated[:, 0] * sine_part + accumulated[:, 1] * cosine
            wavefield = jnp.stack([real_part, imag_part], axis=1)
            raws.append(jnp.sum(real_part, axis=0))
        return (wavefield, raws)

    above_floor_lines, above_unscaled_waves = image_downward(incoming_wave, vertical_slab)
    arriving = from_behind(above_floor_lines, "strip", lateral_count)
    second_bottom, second_raws = image_downward(arriving, jnp.maximum(vertical_slab - 1, 0))
    handed = jnp.where(vertical_slab == 0, above_floor_lines, second_bottom)
    first_section = (vertical_slab > 0).astype(jnp.float32)
    totals = [
        above_unscaled_waves[level] + first_section * second_raws[level] for level in range(LEVELS)
    ]
    selector = (jnp.arange(SECTIONS, dtype=jnp.int32) == vertical_slab).astype(jnp.float32)
    images = []
    for level in range(LEVELS):
        raw_image = totals[level]
        spread = lax.psum(selector * jnp.sum(raw_image * raw_image), "strip")
        mean_square = jnp.sum(spread * selector) / section_cells
        images.append(raw_image / jnp.sqrt(mean_square + 1e-06))
    return (jnp.stack(images, axis=0), handed)


LANES = 128
SUB = 8


def cell(i, j):
    return (j, pl.ds(SUB * i, SUB), slice(None))


def column(j):
    return pl.ds(LANES * j, LANES)


def rim(src, plane, tiles):
    sub = lax.broadcasted_iota(jnp.int32, (SUB, LANES), 0)
    lower, upper, rows = [], [], []
    for j in range(tiles):
        v0 = src[(plane,) + cell(0, j)]
        v7 = src[(plane,) + cell(SUB - 1, j)]
        p = v7 + jnp.where(sub == SUB - 1, 0.0, pltpu.roll(v0, SUB - 1, 0))
        lower.append(p)
        upper.append(jnp.where(sub == 0, v0, pltpu.roll(p, 1, 0)))
        rows.append(v0)
    return lower, upper, rows


def across(w):
    lane = lax.broadcasted_iota(jnp.int32, (SUB, LANES), 1)
    tiles = len(w)
    q = [w[j] + w[j + 1] for j in range(tiles - 1)]
    q.append(w[-1] + jnp.where(lane == LANES - 1, 0.0, pltpu.roll(w[0], LANES - 1, 1)))
    before = jnp.where(lane == 0, w[0], pltpu.roll(q[-1], 1, 1))
    return [q[j] + (q[j - 1] if j else before) for j in range(tiles)]


def weighted(table, cells, k, i, j):
    index = cells[cell(i, j)]
    return (
        jnp.take_along_axis(table[k, 0], index, axis=1),
        jnp.take_along_axis(table[k, 1], index, axis=1),
    )


def advance(src, other, total, cells, table, k, tiles, first=False, mac=False):
    edges = [rim(src, plane, tiles) for plane in range(2)]
    above = [e[1] for e in edges]
    present = [e[2] for e in edges]
    for i in range(SUB):
        new, old = [], []
        for plane in range(2):
            if i < SUB - 1:
                below = [src[(plane,) + cell(i + 1, j)] for j in range(tiles)]
                pairs = [present[plane][j] + below[j] for j in range(tiles)]
            else:
                below = None
                pairs = edges[plane][0]
            h = across([pairs[j] + above[plane][j] for j in range(tiles)])
            above[plane] = pairs
            out = []
            for j in range(tiles):
                at = (plane,) + cell(i, j)
                v = present[plane][j]
                u = v - 0.125 * h[j] if first else (v + v) - (0.25 * h[j] + other[at])
                other[at] = u
                out.append(u)
            old.append(present[plane])
            present[plane] = below
            new.append(out)
        if mac:
            for j in range(tiles):
                c0r, c0i = weighted(table, cells, k, i, j)
                c1r, c1i = weighted(table, cells, k + 1, i, j)
                ur, ui = new[0][j], new[1][j]
                vr, vi = old[0][j], old[1][j]
                a = (c1r * ur - c1i * ui) + (c0r * vr - c0i * vi)
                b = (c1r * ui + c1i * ur) + (c0r * vi + c0i * vr)
                re, im = (0,) + cell(i, j), (1,) + cell(i, j)
                if first:
                    total[re], total[im] = a, b
                else:
                    total[re] = total[re] + a
                    total[im] = total[im] + b


def one_level(src, even, odd, total, cells, table, tiles):
    advance(src, odd, total, cells, table, 0, tiles, first=True, mac=True)
    for plane in range(2):
        for i in range(SUB):
            for j in range(tiles):
                even[(plane,) + cell(i, j)] = src[(plane,) + cell(i, j)]

    def pair(t, carry):
        k = 2 * t + 1
        advance(odd, even, total, cells, table, k, tiles)
        advance(even, odd, total, cells, table, k + 1, tiles, mac=True)
        return carry

    lax.fori_loop(0, ORDER // 2 - 1, pair, 0)
    advance(odd, even, total, cells, table, ORDER - 1, tiles)
    for i in range(SUB):
        for j in range(tiles):
            cr, ci = weighted(table, cells, ORDER, i, j)
            re, im = (0,) + cell(i, j), (1,) + cell(i, j)
            ur, ui = even[re], even[im]
            total[re] = total[re] + (cr * ur - ci * ui)
            total[im] = total[im] + (cr * ui + ci * ur)


def fold(block, turned, tiles):
    for j in range(tiles):
        turned[column(j), :] = block[:, column(j)].T
    return [turned[pl.ds(j, LANES, stride=tiles), :].T for j in range(tiles)]


def unfold(block, turned, tiles):
    for j in range(tiles):
        turned[pl.ds(j, LANES, stride=tiles), :] = block[:, column(j)].T
    return [turned[column(j), :].T for j in range(tiles)]


def folded_cells(lane_ref, own, across_chip, core_pair, natural, block, turned, cells, tiles):
    here = lane_ref[0]
    rows = own.shape[2]
    strips = (here ^ 2, here, here ^ 3, here ^ 1)
    pieces = (own, across_chip, core_pair.at[0], core_pair.at[1])
    for piece, strip in zip(pieces, strips):
        at = pl.ds(pl.multiple_of(strip * rows, rows), rows)
        for level in range(LEVELS):
            for which in range(2):
                for j in range(tiles):
                    natural[which * LEVELS + level, j, at, :] = piece[which, level, :, column(j)]
    for which in range(2):
        for level in range(LEVELS):
            for i in range(SUB):
                for j in range(tiles):
                    block[pl.ds(64 * level + SUB * i, SUB), column(j)] = natural[
                        which * LEVELS + level, j, pl.ds(i, SUB, stride=SUB), :
                    ].astype(jnp.float32)
        for j, tile in enumerate(fold(block, turned, tiles)):
            for level in range(LEVELS):
                cells[which * LEVELS + level, j] = tile[64 * level : 64 * level + 64].astype(
                    jnp.int32
                )


def cells_kernel(lane_ref, own, across_chip, core_pair, cells, natural, block, turned):
    folded_cells(
        lane_ref, own, across_chip, core_pair, natural, block, turned, cells, cells.shape[1]
    )


def rows_out(level_total, bottom, natural, outs, here, rows):
    for j in range(bottom.shape[1]):
        for g in range(SUB):
            at = pl.ds(SUB * g, SUB)
            natural[0, j, at, :] = level_total[0, j, pl.ds(g, SUB, stride=SUB), :]
            natural[1, j, at, :] = bottom[0, j, pl.ds(g, SUB, stride=SUB), :]
            natural[2, j, at, :] = bottom[1, j, pl.ds(g, SUB, stride=SUB), :]
    for r, out in enumerate(outs):
        at = pl.ds(pl.multiple_of((here ^ r ^ 2) * rows, rows), rows)
        for plane in range(3):
            for j in range(bottom.shape[1]):
                out[plane, :, column(j)] = natural[plane, j, at, :]


def upper_kernel(
    lane_ref, w0, w1, w2, w3, cells, table, bottom, o0, o1, o2, o3, first, even, odd, block, turned, natural
):
    here = lane_ref[0]
    rows = w0.shape[1]
    tiles = w0.shape[2] // LANES
    for r, piece in enumerate((w0, w1, w2, w3)):
        at = pl.ds(pl.multiple_of((here ^ r ^ 2) * rows, rows), rows)
        for plane in range(2):
            for j in range(tiles):
                natural[plane, j, at, :] = piece[plane, :, column(j)]
    for plane in range(2):
        for i in range(SUB):
            for j in range(tiles):
                block[pl.ds(64 * plane + SUB * i, SUB), column(j)] = natural[
                    plane, j, pl.ds(i, SUB, stride=SUB), :
                ]
    for j, tile in enumerate(fold(block, turned, tiles)):
        for plane in range(2):
            bottom[plane, j] = tile[64 * plane : 64 * plane + 64]
    one_level(bottom, even, odd, first, cells.at[0], table, tiles)
    one_level(first, even, odd, bottom, cells.at[1], table, tiles)
    rows_out(first, bottom, natural, (o0, o1, o2, o3), here, rows)


def lower_kernel(lane_ref, wave, cells, table, o0, o1, o2, o3, first, second, even, odd, natural):
    here = lane_ref[0]
    tiles = wave.shape[1]
    one_level(wave, even, odd, first, cells.at[LEVELS], table, tiles)
    one_level(first, even, odd, second, cells.at[LEVELS + 1], table, tiles)
    rows_out(first, second, natural, (o0, o1, o2, o3), here, o0.shape[1])


def final_kernel(
    lane_ref, m0, m1, m2, m3, n0, n1, n2, n3, handed, raw, squares, block, turned, picture
):
    here, top = lane_ref[0], lane_ref[1] == 0
    rows = m0.shape[1]
    tiles = m0.shape[2] // LANES
    sums = []
    for level in range(LEVELS):
        early = (n0[level] + n1[level]) + (n2[level] + n3[level])
        late = (m0[level] + m1[level]) + (m2[level] + m3[level])
        total = jnp.where(top, early, early + late)
        picture[pl.ds(rows * level, rows), :] = total
        sums.append(jnp.sum(total * total))
    lane = lax.broadcasted_iota(jnp.int32, (SUB, LANES), 1)
    squares[...] = jnp.where(lane == 0, sums[0], jnp.where(lane == 1, sums[1], 0.0))
    for r, (m, n) in enumerate(zip((m0, m1, m2, m3), (n0, n1, n2, n3))):
        at = (here ^ r) * (2 * rows)
        for plane in range(2):
            block[pl.ds(pl.multiple_of(at + plane * rows, rows), rows), :] = jnp.where(
                top, n[1 + plane], m[1 + plane]
            )
    for j, tile in enumerate(unfold(block, turned, tiles)):
        for f in range(NFREQ):
            for plane in range(2):
                start = (2 * f + plane) * rows
                handed[f, plane, :, column(j)] = tile[start : start + rows]
    for j, tile in enumerate(unfold(picture, turned, tiles)):
        for level in range(LEVELS):
            raw[level, :, column(j)] = tile[rows * level : rows * level + rows]


def call(kernel, outs, scratch, *operands):
    vmem = pl.BlockSpec(memory_space=pltpu.VMEM)
    smem = pl.BlockSpec(memory_space=pltpu.SMEM)
    return pl.pallas_call(
        kernel,
        out_shape=outs,
        in_specs=[smem] + [vmem] * (len(operands) - 1),
        out_specs=[vmem] * len(outs),
        scratch_shapes=scratch,
        compiler_params=pltpu.CompilerParams(vmem_limit_bytes=40 << 20),
    )(*operands)


def frequency_shards(
    incoming_wave,
    speed_class_map,
    spectral_entry_index,
    filter_weights,
    scaled_pulsations,
    inverse_speed_classes,
):
    devices = lax.axis_size("strip")
    rows, columns = incoming_wave.shape[2], incoming_wave.shape[3]
    me = lax.axis_index("strip")
    plane, here = me // NFREQ, me % NFREQ
    planes = devices // NFREQ

    def place(p, lane):
        return (p % planes) * NFREQ + lane

    everyone = [(p, lane) for p in range(planes) for lane in range(NFREQ)]

    def send(value, pairs):
        return lax.ppermute(value, "strip", pairs)

    far = send(
        speed_class_map,
        [(place(p, lane), place(p + (1 if lane >= 2 else -1), lane)) for p, lane in everyone],
    )
    starts = [
        send(
            lax.dynamic_index_in_dim(incoming_wave, here ^ r, 0, keepdims=False),
            [(place(p, lane), place(p + lane // 2, lane ^ r)) for p, lane in everyone],
        )
        for r in range(NFREQ)
    ]
    upper_half = here >= 2
    own = jnp.stack(
        [
            jnp.where(upper_half, far, speed_class_map),
            jnp.where(upper_half, speed_class_map, far),
        ]
    )
    across_chip = send(own, [(place(p, lane), place(p, lane ^ 2)) for p, lane in everyone])
    core_pair = send(
        jnp.stack([own, across_chip]), [(place(p, lane), place(p, lane ^ 1)) for p, lane in everyone]
    )

    section = (plane - 1) % planes
    entry = spectral_entry_index[section, here]
    weights = lax.dynamic_index_in_dim(filter_weights, entry, 0, keepdims=False)
    pulsation = scaled_pulsations[entry]
    angle = pulsation * inverse_speed_classes
    cosine, sine = jnp.cos(angle)[:, None], jnp.sin(angle)[:, None]
    sign = 1.0 - 2.0 * (jnp.arange(ORDER + 1) % 2).astype(jnp.float32)
    real = (weights[:, 0] * cosine - weights[:, 1] * sine) * sign
    imag = (weights[:, 0] * sine + weights[:, 1] * cosine) * sign
    table = jnp.stack([real, imag], axis=0).transpose(2, 0, 1)
    table = jnp.pad(table, ((0, 0), (0, 0), (0, LANES - NBIN)))
    table = jnp.broadcast_to(table[:, :, None, :], (ORDER + 1, 2, SUB, LANES))

    owned = (plane - jnp.where(upper_half, 0, 1)) % planes
    lanes = jnp.stack([here, owned]).astype(jnp.int32)
    field = (2, columns // LANES, SUB * SUB, LANES)
    natural = pltpu.VMEM((3,) + field[1:], jnp.float32)
    half = pltpu.VMEM(field, jnp.float32)
    turned = pltpu.VMEM((columns, LANES), jnp.float32)
    block = pltpu.VMEM((LANES, columns), jnp.float32)
    shape = jax.ShapeDtypeStruct
    message = shape((3, rows, columns), jnp.float32)

    (cells,) = call(
        cells_kernel,
        [shape((2 * LEVELS,) + field[1:], jnp.int32)],
        [pltpu.VMEM((2 * LEVELS,) + field[1:], jnp.int32), block, turned],
        lanes,
        own,
        across_chip,
        core_pair,
    )
    bottom, *early = call(
        upper_kernel,
        [shape(field, jnp.float32)] + [message] * NFREQ,
        [half, half, half, block, turned, natural],
        lanes,
        *starts,
        cells,
        table,
    )
    early = [
        send(v, [(place(p, lane), place(p - (lane ^ r) // 2, lane ^ r)) for p, lane in everyone])
        for r, v in enumerate(early)
    ]
    late = call(
        lower_kernel,
        [message] * NFREQ,
        [half, half, half, half, natural],
        lanes,
        bottom,
        cells,
        table,
    )
    late = [
        send(v, [(place(p, lane), place(p + 1 - (lane ^ r) // 2, lane ^ r)) for p, lane in everyone])
        for r, v in enumerate(late)
    ]
    handed, raw, squares = call(
        final_kernel,
        [
            shape(incoming_wave.shape, jnp.float32),
            shape(speed_class_map.shape, jnp.float32),
            shape((SUB, LANES), jnp.float32),
        ],
        [block, turned, block],
        lanes,
        *late,
        *early,
    )

    def owner(s, strip):
        return place(s + strip // 2, strip ^ 2)

    mean_square = squares
    for r in range(1, NFREQ):
        mean_square = mean_square + send(
            squares,
            [(owner(s, strip), owner(s, strip ^ r)) for s in range(planes) for strip in range(NFREQ)],
        )
    mean_square = mean_square[0, :LEVELS] / (rows * NFREQ * columns)
    image = raw / jnp.sqrt(mean_square + 1e-06)[:, None, None]
    return (image, handed)


def shards(*operands):
    lateral_count = lax.axis_size("strip") // SECTIONS
    rows, columns = operands[0].shape[2:]
    if lateral_count == NFREQ and rows * lateral_count == SUB * SUB and columns == SUB * LANES:
        return frequency_shards(*operands)
    return strip_shards(*operands)


def solution(mesh):
    return jax.shard_map(
        shards,
        mesh=mesh,
        in_specs=(
            P("groups", None, "strip", None),
            P("groups", "strip", None),
            P("groups", None),
            P(),
            P(),
            P(),
        ),
        out_specs=(P("groups", "strip", None), P("groups", None, "strip", None)),
        check_vma=False,
    )
```

profile of v0, /device:TPU:0, one launch (start us, length us, event | category | flops | bytes accessed | tf_op | source)
XLA Modules:
  0.0 88.0 jit_solution(4043113869179952419)
XLA Ops:
  0.6 5.1 %collective-permute-start.4 = (s32[2,16,1024]{2,1,0:T(8,128)}, s32[2,16,1024]{2,1,0:T(8,128)S(1)}, u32[]{:S(2)}, u32[]{:S(2)}) collective-permute-start(s32[2,16,1024]{2,1,0:T(8,128)} %param.7), channel_id=1, source_target_pairs={{0,12},{1,13},{2,6},{3,7},{4,0},{5,1},{6,10},{7,11},{8,4},{9,5},{1... | collective-permute-start | bytes 393224 | tf_op jit(solution)/shard_map/ppermute | solution.py:414
  5.7 1.2 %dynamic-slice_bitcast_fusion = (f32[2,16,1024]{2,1,0:T(8,128)S(1)}, f32[2,16,1024]{2,1,0:T(8,128)S(1)}, f32[2,16,1024]{2,1,0:T(8,128)S(1)}, f32[2,16,1024]{2,1,0:T(8,128)S(1)}) fusion(f32[4,2,16,1024]{3,2,1,0:T(8,128)} %param.6, s32[]{:T(128)S(6)} %select_n.76, s32[]{:T(128)S(6)} %select_n.74, s32[]{:T(128)S(6)} %select_n.73, s32[]{:T(128)S(6)} %select_n.75), kind=kLoop, calls=%fused_computation.4 | loop fusion | bytes 1048592 | tf_op jit(solution)/shard_map/jit(dynamic_index_in_dim)/squeeze | solution.py:422
  7.1 0.7 collective-permute-start
  7.7 4.0 %collective-permute-start.2 = (f32[2,16,1024]{2,1,0:T(8,128)S(1)}, f32[2,16,1024]{2,1,0:T(8,128)S(1)}, u32[]{:S(2)}, u32[]{:S(2)}) collective-permute-start(f32[2,16,1024]{2,1,0:T(8,128)S(1)} %get-tuple-element.29), channel_id=1, source_target_pairs={{0,2},{1,3},{2,4},{3,5},{4,6},{5,7},{6,8},{7,9},{8,10},{9,11},{10,... | collective-permute-start | bytes 393224 | tf_op jit(solution)/shard_map/ppermute | solution.py:414
  11.7 1.3 %dynamic_slice.27 = s32[1,1]{1,0:T(1,128)} dynamic-slice(s32[4,4]{1,0:T(4,128)} %param.8, s32[]{:T(128)S(6)} %select_n.81, s32[]{:T(128)S(6)} %select_n.73), dynamic_slice_sizes={1,1} | dynamic-slice | bytes 12 | tf_op jit(solution)/shard_map/dynamic_slice | solution.py:440
  15.2 0.5 copy-done.3
  15.7 0.6 dynamic_slice.29
  16.3 0.7 copy-done.2
  16.9 0.7 multiply_cosine_fusion
  17.6 8.0 %collective-permute-done.5.across_chip = s32[2,2,16,1024]{3,2,1,0:T(8,128)S(1)} collective-permute-done((s32[2,2,16,1024]{3,2,1,0:T(8,128)S(1)}, s32[2,2,16,1024]{3,2,1,0:T(8,128)S(1)}, u32[]{:S(2)}, u32[]{:S(2)}) %collective-permute-start.5) | collective-permute-done | bytes 262176 | tf_op jit(solution)/shard_map/ppermute | solution.py:414
  26.0 1.7 %collective-permute-done.6.core_pair = s32[2,2,2,16,1024]{4,3,2,1,0:T(8,128)S(1)} collective-permute-done((s32[2,2,2,16,1024]{4,3,2,1,0:T(8,128)S(1)}, s32[2,2,2,16,1024]{4,3,2,1,0:T(8,128)S(1)}, u32[]{:S(2)}, u32[]{:S(2)}) %collective-permute-start.6) | collective-permute-done | bytes 524320 | tf_op jit(solution)/shard_map/ppermute | solution.py:414
  27.6 1.4 %shard_map.77.cells = s32[4,8,64,128]{3,2,1,0:T(8,128)S(1)} custom-call(s32[2]{0:T(128)S(1)} %pad_add_fusion.2.lane_ref, s32[2,2,16,1024]{3,2,1,0:T(8,128)S(1)} %get-tuple-element.31.own, s32[2,2,16,1024]{3,2,1,0:T(8,128)S(1)} %collective-permute-done.5.across_chip, s32[2,2,2,16,1024]{4,3,2,1,0:T(8,128)S(1)} %collective-permute-done.6.core_pair), custom_call_target="tpu_custom_call" | custom-call | tf_op jit(solution)/shard_map/pallas_call | solution.py:384
  29.1 11.2 %shard_map.78 = (f32[2,8,64,128]{3,2,1,0:T(8,128)S(1)}, f32[3,16,1024]{2,1,0:T(8,128)S(1)}, f32[3,16,1024]{2,1,0:T(8,128)S(1)}, f32[3,16,1024]{2,1,0:T(8,128)S(1)}, f32[3,16,1024]{2,1,0:T(8,128)S(1)}) custom-call(s32[2]{0:T(128)S(1)} %pad_add_fusion.2.lane_ref, f32[2,16,1024]{2,1,0:T(8,128)S(1)} %collective-permute-done.w0, ...), custom_call_target="tpu_custom_call" | custom-call | tf_op jit(solution)/shard_map/pallas_call | solution.py:384
  40.3 10.6 %shard_map.79 = (f32[3,16,1024]{2,1,0:T(8,128)S(1)}, f32[3,16,1024]{2,1,0:T(8,128)S(1)}, f32[3,16,1024]{2,1,0:T(8,128)S(1)}, f32[3,16,1024]{2,1,0:T(8,128)S(1)}) custom-call(s32[2]{0:T(128)S(1)} %pad_add_fusion.2.lane_ref, f32[2,8,64,128]{3,2,1,0:T(8,128)S(1)} %get-tuple-element.14.wave, s32[4,8,64,128]{3,2,1,0:T(8,128)S(1)} %shard_map.77.cells, ...), custom_call_target="tpu_custom_call" | custom-call | tf_op jit(solution)/shard_map/pallas_call | solution.py:384
  50.9 3.3 %collective-permute-start.7 = (f32[3,16,1024]{2,1,0:T(8,128)S(1)}, f32[3,16,1024]{2,1,0:T(8,128)S(1)}, u32[]{:S(2)}, u32[]{:S(2)}) collective-permute-start(f32[3,16,1024]{2,1,0:T(8,128)S(1)} %get-tuple-element.15), channel_id=1, source_target_pairs={{0,4},{1,5},{2,2},{3,3},{4,8},{5,9},{6,6},{7,7},{8,12},{9,13},{10,... | collective-permute-start | bytes 589832 | tf_op jit(solution)/shard_map/ppermute | solution.py:414
  54.2 1.1 %collective-permute-start.8 = (f32[3,16,1024]{2,1,0:T(8,128)S(1)}, f32[3,16,1024]{2,1,0:T(8,128)S(1)}, u32[]{:S(2)}, u32[]{:S(2)}) collective-permute-start(f32[3,16,1024]{2,1,0:T(8,128)S(1)} %get-tuple-element.16), channel_id=1, source_target_pairs={{0,5},{1,4},{2,3},{3,2},{4,9},{5,8},{6,7},{7,6},{8,13},{9,12},{10,... | collective-permute-start | bytes 589832 | tf_op jit(solution)/shard_map/ppermute | solution.py:414
  55.3 2.3 %collective-permute-start.10 = (f32[3,16,1024]{2,1,0:T(8,128)S(1)}, f32[3,16,1024]{2,1,0:T(8,128)S(1)}, u32[]{:S(2)}, u32[]{:S(2)}) collective-permute-start(f32[3,16,1024]{2,1,0:T(8,128)S(1)} %get-tuple-element.18), channel_id=1, source_target_pairs={{0,3},{1,2},{2,5},{3,4},{4,7},{5,6},{6,9},{7,8},{8,11},{9,10},{10,... | collective-permute-start | bytes 589832 | tf_op jit(solution)/shard_map/ppermute | solution.py:414
  57.6 0.7 collective-permute-start.11
  58.3 4.1 %collective-permute-done.7.m0 = f32[3,16,1024]{2,1,0:T(8,128)S(1)} collective-permute-done((f32[3,16,1024]{2,1,0:T(8,128)S(1)}, f32[3,16,1024]{2,1,0:T(8,128)S(1)}, u32[]{:S(2)}, u32[]{:S(2)}) %collective-permute-start.7) | collective-permute-done | bytes 196640 | tf_op jit(solution)/shard_map/ppermute | solution.py:414
  62.3 2.6 %collective-permute-done.8.m1 = f32[3,16,1024]{2,1,0:T(8,128)S(1)} collective-permute-done((f32[3,16,1024]{2,1,0:T(8,128)S(1)}, f32[3,16,1024]{2,1,0:T(8,128)S(1)}, u32[]{:S(2)}, u32[]{:S(2)}) %collective-permute-start.8) | collective-permute-done | bytes 196640 | tf_op jit(solution)/shard_map/ppermute | solution.py:414
  64.9 0.9 %collective-permute-done.9.m2 = f32[3,16,1024]{2,1,0:T(8,128)S(1)} collective-permute-done((f32[3,16,1024]{2,1,0:T(8,128)S(1)}, f32[3,16,1024]{2,1,0:T(8,128)S(1)}, u32[]{:S(2)}, u32[]{:S(2)}) %collective-permute-start.9) | collective-permute-done | bytes 196640 | tf_op jit(solution)/shard_map/ppermute | solution.py:414
  65.9 1.7 %collective-permute-start.14 = (f32[3,16,1024]{2,1,0:T(8,128)S(1)}, f32[3,16,1024]{2,1,0:T(8,128)S(1)}, u32[]{:S(2)}, u32[]{:S(2)}) collective-permute-start(f32[3,16,1024]{2,1,0:T(8,128)S(1)} %get-tuple-element.22), channel_id=1, source_target_pairs={{0,15},{1,14},{2,1},{3,0},{4,3},{5,2},{6,5},{7,4},{8,7},{9,6},{10,... | collective-permute-start | bytes 589832 | tf_op jit(solution)/shard_map/ppermute | solution.py:414
  67.6 2.0 %collective-permute-done.10.m3 = f32[3,16,1024]{2,1,0:T(8,128)S(1)} collective-permute-done((f32[3,16,1024]{2,1,0:T(8,128)S(1)}, f32[3,16,1024]{2,1,0:T(8,128)S(1)}, u32[]{:S(2)}, u32[]{:S(2)}) %collective-permute-start.10) | collective-permute-done | bytes 196640 | tf_op jit(solution)/shard_map/ppermute | solution.py:414
  69.6 4.4 %collective-permute-done.13.n2 = f32[3,16,1024]{2,1,0:T(8,128)S(1)} collective-permute-done((f32[3,16,1024]{2,1,0:T(8,128)S(1)}, f32[3,16,1024]{2,1,0:T(8,128)S(1)}, u32[]{:S(2)}, u32[]{:S(2)}) %collective-permute-start.13) | collective-permute-done | bytes 196640 | tf_op jit(solution)/shard_map/ppermute | solution.py:414
  74.0 4.2 %collective-permute-done.14.n3 = f32[3,16,1024]{2,1,0:T(8,128)S(1)} collective-permute-done((f32[3,16,1024]{2,1,0:T(8,128)S(1)}, f32[3,16,1024]{2,1,0:T(8,128)S(1)}, u32[]{:S(2)}, u32[]{:S(2)}) %collective-permute-start.14) | collective-permute-done | bytes 196640 | tf_op jit(solution)/shard_map/ppermute | solution.py:414
  78.2 1.9 %shard_map.80 = (f32[4,2,16,1024]{3,2,1,0:T(8,128)}, f32[2,16,1024]{2,1,0:T(8,128)S(1)}, f32[8,128]{1,0:T(8,128)S(1)}) custom-call(s32[2]{0:T(128)S(1)} %pad_add_fusion.2.lane_ref, f32[3,16,1024]{2,1,0:T(8,128)S(1)} %collective-permute-done.7.m0, f32[3,16,1024]{2,1,0:T(8,128)S(1)} %collective-permute-done.8.m1, ...), custom_call_target="tpu_custom_call" | custom-call | tf_op jit(solution)/shard_map/pallas_call | solution.py:384
  80.1 0.9 %collective-permute-start.17 = (f32[8,128]{1,0:T(8,128)S(1)}, f32[8,128]{1,0:T(8,128)S(1)}, u32[]{:S(2)}, u32[]{:S(2)}) collective-permute-start(f32[8,128]{1,0:T(8,128)S(1)} %get-tuple-element.24), channel_id=1, source_target_pairs={{2,5},{3,4},{4,3},{5,2},{6,9},{7,8},{8,7},{9,6},{10,13},{11,12},{1... | collective-permute-start | bytes 12296 | tf_op jit(solution)/shard_map/ppermute | solution.py:414
  81.0 3.5 %collective-permute-start.16 = (f32[8,128]{1,0:T(8,128)S(1)}, f32[8,128]{1,0:T(8,128)S(1)}, u32[]{:S(2)}, u32[]{:S(2)}) collective-permute-start(f32[8,128]{1,0:T(8,128)S(1)} %get-tuple-element.24), channel_id=1, source_target_pairs={{2,4},{3,5},{4,2},{5,3},{6,8},{7,9},{8,6},{9,7},{10,12},{11,13},{1... | collective-permute-start | bytes 12296 | tf_op jit(solution)/shard_map/ppermute | solution.py:414
  84.5 0.1 collective-permute-start.15
  84.7 1.1 %collective-permute-done.17 = f32[8,128]{1,0:T(8,128)S(1)} collective-permute-done((f32[8,128]{1,0:T(8,128)S(1)}, f32[8,128]{1,0:T(8,128)S(1)}, u32[]{:S(2)}, u32[]{:S(2)}) %collective-permute-start.17) | collective-permute-done | bytes 4128 | tf_op jit(solution)/shard_map/ppermute | solution.py:414
  85.8 1.5 %collective-permute-done.16 = f32[8,128]{1,0:T(8,128)S(1)} collective-permute-done((f32[8,128]{1,0:T(8,128)S(1)}, f32[8,128]{1,0:T(8,128)S(1)}, u32[]{:S(2)}, u32[]{:S(2)}) %collective-permute-start.16) | collective-permute-done | bytes 4128 | tf_op jit(solution)/shard_map/ppermute | solution.py:414
  87.3 0.7 broadcast_divide_fusion
  (33 shorter events, 0.7 us)
Async XLA Ops:
  0.6 14.5 %copy-start = (f32[16,16,2,13]{1,2,3,0:T(2,128)S(1)}, f32[16,16,2,13]{1,2,3,0:T(2,128)}, u32[]{:S(2)}) copy-start(f32[16,16,2,13]{1,2,3,0:T(2,128)} %param.9) | copy-start | bytes 79876
  0.6 14.3 %collective-permute-start.4 = (s32[2,16,1024]{2,1,0:T(8,128)}, s32[2,16,1024]{2,1,0:T(8,128)S(1)}, u32[]{:S(2)}, u32[]{:S(2)}) collective-permute-start(s32[2,16,1024]{2,1,0:T(8,128)} %param.7), channel_id=1, source_target_pairs={{0,12},{1,13},{2,6},{3,7},{4,0},{5,1},{6,10},{7,11},{8,4},{9,5},{1... | collective-permute-start | bytes 393224 | tf_op jit(solution)/shard_map/ppermute | solution.py:414
  5.7 9.2 %copy-start.1 = (s32[2,16,1024]{2,1,0:T(8,128)S(1)}, s32[2,16,1024]{2,1,0:T(8,128)}, u32[]{:S(2)}) copy-start(s32[2,16,1024]{2,1,0:T(8,128)} %param.7) | copy-start | bytes 393220
  6.9 22.1 %collective-permute-start.3 = (f32[2,16,1024]{2,1,0:T(8,128)S(1)}, f32[2,16,1024]{2,1,0:T(8,128)S(1)}, u32[]{:S(2)}, u32[]{:S(2)}) collective-permute-start(f32[2,16,1024]{2,1,0:T(8,128)S(1)} %get-tuple-element.26), channel_id=1, source_target_pairs={{0,3},{1,2},{2,5},{3,4},{4,7},{5,6},{6,9},{7,8},{8,11},{9,10},{10,... | collective-permute-start | bytes 393224 | tf_op jit(solution)/shard_map/ppermute | solution.py:414
  7.0 22.0 %collective-permute-start.1 = (f32[2,16,1024]{2,1,0:T(8,128)S(1)}, f32[2,16,1024]{2,1,0:T(8,128)S(1)}, u32[]{:S(2)}, u32[]{:S(2)}) collective-permute-start(f32[2,16,1024]{2,1,0:T(8,128)S(1)} %get-tuple-element.27), channel_id=1, source_target_pairs={{0,1},{1,0},{2,7},{3,6},{4,5},{5,4},{6,11},{7,10},{8,9},{9,8},{10,... | collective-permute-start | bytes 393224 | tf_op jit(solution)/shard_map/ppermute | solution.py:414
  7.1 22.0 %collective-permute-start = (f32[2,16,1024]{2,1,0:T(8,128)S(1)}, f32[2,16,1024]{2,1,0:T(8,128)S(1)}, u32[]{:S(2)}, u32[]{:S(2)}) collective-permute-start(f32[2,16,1024]{2,1,0:T(8,128)S(1)} %get-tuple-element.28), channel_id=1, source_target_pairs={{0,0},{1,1},{2,6},{3,7},{4,4},{5,5},{6,10},{7,11},{8,8},{9,9},{10,... | collective-permute-start | bytes 393224 | tf_op jit(solution)/shard_map/ppermute | solution.py:414
  7.7 21.3 %collective-permute-start.2 = (f32[2,16,1024]{2,1,0:T(8,128)S(1)}, f32[2,16,1024]{2,1,0:T(8,128)S(1)}, u32[]{:S(2)}, u32[]{:S(2)}) collective-permute-start(f32[2,16,1024]{2,1,0:T(8,128)S(1)} %get-tuple-element.29), channel_id=1, source_target_pairs={{0,2},{1,3},{2,4},{3,5},{4,6},{5,7},{6,8},{7,9},{8,10},{9,11},{10,... | collective-permute-start | bytes 393224 | tf_op jit(solution)/shard_map/ppermute | solution.py:414
  15.0 0.7 copy-start.3
  15.0 10.6 %collective-permute-start.5 = (s32[2,2,16,1024]{3,2,1,0:T(8,128)S(1)}, s32[2,2,16,1024]{3,2,1,0:T(8,128)S(1)}, u32[]{:S(2)}, u32[]{:S(2)}) collective-permute-start(s32[2,2,16,1024]{3,2,1,0:T(8,128)S(1)} %get-tuple-element.31.own), channel_id=1, source_target_pairs={{0,2},{1,3},{2,0},{3,1},{4,6},{5,7},{6,4},{7,5},{8,10},{9,11},{10,... | collective-permute-start | bytes 786440 | tf_op jit(solution)/shard_map/ppermute | solution.py:414
  16.3 0.7 copy-start.2
  25.7 2.0 %collective-permute-start.6 = (s32[2,2,2,16,1024]{4,3,2,1,0:T(8,128)S(1)}, s32[2,2,2,16,1024]{4,3,2,1,0:T(8,128)S(1)}, u32[]{:S(2)}, u32[]{:S(2)}) collective-permute-start(s32[2,2,2,16,1024]{4,3,2,1,0:T(8,128)S(1)} %pad_add_fusion), channel_id=1, source_target_pairs={{0,1},{1,0},{2,3},{3,2},{4,5},{5,4},{6,7},{7,6},{8,9},{9,8},{10,11... | collective-permute-start | bytes 1572872 | tf_op jit(solution)/shard_map/ppermute | solution.py:414
  50.9 11.4 %collective-permute-start.7 = (f32[3,16,1024]{2,1,0:T(8,128)S(1)}, f32[3,16,1024]{2,1,0:T(8,128)S(1)}, u32[]{:S(2)}, u32[]{:S(2)}) collective-permute-start(f32[3,16,1024]{2,1,0:T(8,128)S(1)} %get-tuple-element.15), channel_id=1, source_target_pairs={{0,4},{1,5},{2,2},{3,3},{4,8},{5,9},{6,6},{7,7},{8,12},{9,13},{10,... | collective-permute-start | bytes 589832 | tf_op jit(solution)/shard_map/ppermute | solution.py:414
  54.2 10.8 %collective-permute-start.8 = (f32[3,16,1024]{2,1,0:T(8,128)S(1)}, f32[3,16,1024]{2,1,0:T(8,128)S(1)}, u32[]{:S(2)}, u32[]{:S(2)}) collective-permute-start(f32[3,16,1024]{2,1,0:T(8,128)S(1)} %get-tuple-element.16), channel_id=1, source_target_pairs={{0,5},{1,4},{2,3},{3,2},{4,9},{5,8},{6,7},{7,6},{8,13},{9,12},{10,... | collective-permute-start | bytes 589832 | tf_op jit(solution)/shard_map/ppermute | solution.py:414
  55.3 10.6 %collective-permute-start.9 = (f32[3,16,1024]{2,1,0:T(8,128)S(1)}, f32[3,16,1024]{2,1,0:T(8,128)S(1)}, u32[]{:S(2)}, u32[]{:S(2)}) collective-permute-start(f32[3,16,1024]{2,1,0:T(8,128)S(1)} %get-tuple-element.17), channel_id=1, source_target_pairs={{0,2},{1,3},{2,4},{3,5},{4,6},{5,7},{6,8},{7,9},{8,10},{9,11},{10,... | collective-permute-start | bytes 589832 | tf_op jit(solution)/shard_map/ppermute | solution.py:414
  55.3 14.3 %collective-permute-start.10 = (f32[3,16,1024]{2,1,0:T(8,128)S(1)}, f32[3,16,1024]{2,1,0:T(8,128)S(1)}, u32[]{:S(2)}, u32[]{:S(2)}) collective-permute-start(f32[3,16,1024]{2,1,0:T(8,128)S(1)} %get-tuple-element.18), channel_id=1, source_target_pairs={{0,3},{1,2},{2,5},{3,4},{4,7},{5,6},{6,9},{7,8},{8,11},{9,10},{10,... | collective-permute-start | bytes 589832 | tf_op jit(solution)/shard_map/ppermute | solution.py:414
  57.6 12.0 %collective-permute-start.11 = (f32[3,16,1024]{2,1,0:T(8,128)S(1)}, f32[3,16,1024]{2,1,0:T(8,128)S(1)}, u32[]{:S(2)}, u32[]{:S(2)}) collective-permute-start(f32[3,16,1024]{2,1,0:T(8,128)S(1)} %get-tuple-element.19), channel_id=1, source_target_pairs={{0,0},{1,1},{2,14},{3,15},{4,4},{5,5},{6,2},{7,3},{8,8},{9,9},{10,... | collective-permute-start | bytes 589832 | tf_op jit(solution)/shard_map/ppermute | solution.py:414
  62.3 7.2 %collective-permute-start.12 = (f32[3,16,1024]{2,1,0:T(8,128)S(1)}, f32[3,16,1024]{2,1,0:T(8,128)S(1)}, u32[]{:S(2)}, u32[]{:S(2)}) collective-permute-start(f32[3,16,1024]{2,1,0:T(8,128)S(1)} %get-tuple-element.20), channel_id=1, source_target_pairs={{0,1},{1,0},{2,15},{3,14},{4,5},{5,4},{6,3},{7,2},{8,9},{9,8},{10,... | collective-permute-start | bytes 589832 | tf_op jit(solution)/shard_map/ppermute | solution.py:414
  64.9 9.1 %collective-permute-start.13 = (f32[3,16,1024]{2,1,0:T(8,128)S(1)}, f32[3,16,1024]{2,1,0:T(8,128)S(1)}, u32[]{:S(2)}, u32[]{:S(2)}) collective-permute-start(f32[3,16,1024]{2,1,0:T(8,128)S(1)} %get-tuple-element.21), channel_id=1, source_target_pairs={{0,14},{1,15},{2,0},{3,1},{4,2},{5,3},{6,4},{7,5},{8,6},{9,7},{10,... | collective-permute-start | bytes 589832 | tf_op jit(solution)/shard_map/ppermute | solution.py:414
  65.9 12.3 %collective-permute-start.14 = (f32[3,16,1024]{2,1,0:T(8,128)S(1)}, f32[3,16,1024]{2,1,0:T(8,128)S(1)}, u32[]{:S(2)}, u32[]{:S(2)}) collective-permute-start(f32[3,16,1024]{2,1,0:T(8,128)S(1)} %get-tuple-element.22), channel_id=1, source_target_pairs={{0,15},{1,14},{2,1},{3,0},{4,3},{5,2},{6,5},{7,4},{8,7},{9,6},{10,... | collective-permute-start | bytes 589832 | tf_op jit(solution)/shard_map/ppermute | solution.py:414
  80.1 5.7 %collective-permute-start.17 = (f32[8,128]{1,0:T(8,128)S(1)}, f32[8,128]{1,0:T(8,128)S(1)}, u32[]{:S(2)}, u32[]{:S(2)}) collective-permute-start(f32[8,128]{1,0:T(8,128)S(1)} %get-tuple-element.24), channel_id=1, source_target_pairs={{2,5},{3,4},{4,3},{5,2},{6,9},{7,8},{8,7},{9,6},{10,13},{11,12},{1... | collective-permute-start | bytes 12296 | tf_op jit(solution)/shard_map/ppermute | solution.py:414
  81.0 6.3 %collective-permute-start.16 = (f32[8,128]{1,0:T(8,128)S(1)}, f32[8,128]{1,0:T(8,128)S(1)}, u32[]{:S(2)}, u32[]{:S(2)}) collective-permute-start(f32[8,128]{1,0:T(8,128)S(1)} %get-tuple-element.24), channel_id=1, source_target_pairs={{2,4},{3,5},{4,2},{5,3},{6,8},{7,9},{8,6},{9,7},{10,12},{11,13},{1... | collective-permute-start | bytes 12296 | tf_op jit(solution)/shard_map/ppermute | solution.py:414
  84.5 2.8 %collective-permute-start.15 = (f32[8,128]{1,0:T(8,128)S(1)}, f32[8,128]{1,0:T(8,128)S(1)}, u32[]{:S(2)}, u32[]{:S(2)}) collective-permute-start(f32[8,128]{1,0:T(8,128)S(1)} %get-tuple-element.24), channel_id=1, source_target_pairs={{2,3},{3,2},{4,5},{5,4},{6,7},{7,6},{8,9},{9,8},{10,11},{11,10},{1... | collective-permute-start | bytes 12296 | tf_op jit(solution)/shard_map/ppermute | solution.py:414
where the time goes:
time: 88.3 us; the launch traced here: 88 us
  waiting for transfers between devices  30.5 us (35%)
  Pallas kernels  25 us (28%)
  starting transfers between devices  23.7 us (27%)
  local copies, waits for them, and re-layouts  4.22 us (5%)
  between operations  2.82 us (3%)
  other arithmetic  1.74 us (2%)
    ppermute x18, waiting for transfers between devices, send(): return lax.ppermute(value, 'strip', pairs)  30.5 us
    pallas_call x4, Pallas kernels, call(): pl.pallas_call(kernel, out_shape=outs, in_specs=[smem] + [vmem] * (len(op...  25 us
    ppermute x18, starting transfers between devices, send(): return lax.ppermute(value, 'strip', pairs)  23.7 us
  transfers between devices with their start and end apart: 18, of which 10 were waited for; matrix products, arithmetic and copies ran while one was open for 5% of the time, Pallas kernels for 2%

commit v1 on v0

--- a/solution.py
+++ b/solution.py
@@ -269,35 +269,29 @@
     return [turned[column(j), :].T for j in range(tiles)]
 
 
-def folded_cells(lane_ref, own, across_chip, core_pair, natural, block, turned, cells, tiles):
+def cells_kernel(lane_ref, own, two, one, three, cells, natural, block, turned):
     here = lane_ref[0]
-    rows = own.shape[2]
+    tiles = cells.shape[1]
+    rows = own.shape[1]
     strips = (here ^ 2, here, here ^ 3, here ^ 1)
-    pieces = (own, across_chip, core_pair.at[0], core_pair.at[1])
-    for piece, strip in zip(pieces, strips):
+    for piece, strip in zip((own, two, one, three), strips):
         at = pl.ds(pl.multiple_of(strip * rows, rows), rows)
         for level in range(LEVELS):
-            for which in range(2):
-                for j in range(tiles):
-                    natural[which * LEVELS + level, j, at, :] = piece[which, level, :, column(j)]
-    for which in range(2):
+            for j in range(tiles):
+                natural[level, j, at, :] = piece[level, :, column(j)]
+    for level in range(LEVELS):
+        for i in range(SUB):
+            for j in range(tiles):
+                block[pl.ds(64 * level + SUB * i, SUB), column(j)] = natural[
+                    level, j, pl.ds(i, SUB, stride=SUB), :
+                ].astype(jnp.float32)
+    for j, tile in enumerate(fold(block, turned, tiles)):
         for level in range(LEVELS):
-            for i in range(SUB):
-                for j in range(tiles):
-                    block[pl.ds(64 * level + SUB * i, SUB), column(j)] = natural[
-                        which * LEVELS + level, j, pl.ds(i, SUB, stride=SUB), :
-                    ].astype(jnp.float32)
-        for j, tile in enumerate(fold(block, turned, tiles)):
-            for level in range(LEVELS):
-                cells[which * LEVELS + level, j] = tile[64 * level : 64 * level + 64].astype(
-                    jnp.int32
-                )
-
-
-def cells_kernel(lane_ref, own, across_chip, core_pair, cells, natural, block, turned):
-    folded_cells(
-        lane_ref, own, across_chip, core_pair, natural, block, turned, cells, cells.shape[1]
-    )
+            cells[level, j] = tile[64 * level : 64 * level + 64].astype(jnp.int32)
+
+
+def paired_cells_kernel(lane_ref, own, two, pair, *refs):
+    cells_kernel(lane_ref, own, two, pair.at[0], pair.at[1], *refs)
 
 
 def rows_out(level_total, bottom, natural, outs, here, rows):
@@ -315,7 +309,8 @@
 
 
 def upper_kernel(
-    lane_ref, w0, w1, w2, w3, cells, table, bottom, o0, o1, o2, o3, first, even, odd, block, turned, natural
+    lane_ref, w0, w1, w2, w3, cells, table, bottom, o0, o1, o2, o3,
+    first, even, odd, block, turned, natural,
 ):
     here = lane_ref[0]
     rows = w0.shape[1]
@@ -342,15 +337,13 @@
 def lower_kernel(lane_ref, wave, cells, table, o0, o1, o2, o3, first, second, even, odd, natural):
     here = lane_ref[0]
     tiles = wave.shape[1]
-    one_level(wave, even, odd, first, cells.at[LEVELS], table, tiles)
-    one_level(first, even, odd, second, cells.at[LEVELS + 1], table, tiles)
+    one_level(wave, even, odd, first, cells.at[0], table, tiles)
+    one_level(first, even, odd, second, cells.at[1], table, tiles)
     rows_out(first, second, natural, (o0, o1, o2, o3), here, o0.shape[1])
 
 
-def final_kernel(
-    lane_ref, m0, m1, m2, m3, n0, n1, n2, n3, handed, raw, squares, block, turned, picture
-):
-    here, top = lane_ref[0], lane_ref[1] == 0
+def image_kernel(lane_ref, m0, m1, m2, m3, n0, n1, n2, n3, raw, squares, turned, picture):
+    top = lane_ref[1] == 0
     rows = m0.shape[1]
     tiles = m0.shape[2] // LANES
     sums = []
@@ -362,6 +355,16 @@
         sums.append(jnp.sum(total * total))
     lane = lax.broadcasted_iota(jnp.int32, (SUB, LANES), 1)
     squares[...] = jnp.where(lane == 0, sums[0], jnp.where(lane == 1, sums[1], 0.0))
+    for level in range(LEVELS):
+        raw[level] = picture[pl.ds(rows * level, rows), :]
+
+
+def handed_kernel(
+    lane_ref, m0, m1, m2, m3, n0, n1, n2, n3, raw, handed, image, block, turned, picture
+):
+    here, top = lane_ref[0], lane_ref[1] == 0
+    rows = m0.shape[1]
+    tiles = m0.shape[2] // LANES
     for r, (m, n) in enumerate(zip((m0, m1, m2, m3), (n0, n1, n2, n3))):
         at = (here ^ r) * (2 * rows)
         for plane in range(2):
@@ -373,12 +376,14 @@
             for plane in range(2):
                 start = (2 * f + plane) * rows
                 handed[f, plane, :, column(j)] = tile[start : start + rows]
+    for level in range(LEVELS):
+        picture[pl.ds(rows * level, rows), :] = raw[level]
     for j, tile in enumerate(unfold(picture, turned, tiles)):
         for level in range(LEVELS):
-            raw[level, :, column(j)] = tile[rows * level : rows * level + rows]
-
-
-def call(kernel, outs, scratch, *operands):
+            image[level, :, column(j)] = tile[rows * level : rows * level + rows]
+
+
+def call(kernel, outs, scratch, operands, moved=0):
     vmem = pl.BlockSpec(memory_space=pltpu.VMEM)
     smem = pl.BlockSpec(memory_space=pltpu.SMEM)
     return pl.pallas_call(
@@ -388,6 +393,7 @@
         out_specs=[vmem] * len(outs),
         scratch_shapes=scratch,
         compiler_params=pltpu.CompilerParams(vmem_limit_bytes=40 << 20),
+        cost_estimate=pl.CostEstimate(flops=moved // 4, bytes_accessed=moved, transcendentals=0),
     )(*operands)
 
 
@@ -413,28 +419,44 @@
     def send(value, pairs):
         return lax.ppermute(value, "strip", pairs)
 
+    def in_plane(r):
+        return [(place(p, n), place(p, n ^ r)) for p, n in everyone]
+
+    def shifted(r):
+        return [(place(p, n), place(p + n // 2, n ^ r)) for p, n in everyone]
+
     far = send(
         speed_class_map,
         [(place(p, lane), place(p + (1 if lane >= 2 else -1), lane)) for p, lane in everyone],
     )
-    starts = [
-        send(
-            lax.dynamic_index_in_dim(incoming_wave, here ^ r, 0, keepdims=False),
-            [(place(p, lane), place(p + lane // 2, lane ^ r)) for p, lane in everyone],
-        )
-        for r in range(NFREQ)
-    ]
+    waves = [lax.dynamic_index_in_dim(incoming_wave, here ^ r, 0, keepdims=False) for r in range(NFREQ)]
+    starts = [send(waves[r], shifted(r)) for r in (0, 1)]
     upper_half = here >= 2
-    own = jnp.stack(
-        [
-            jnp.where(upper_half, far, speed_class_map),
-            jnp.where(upper_half, speed_class_map, far),
-        ]
-    )
-    across_chip = send(own, [(place(p, lane), place(p, lane ^ 2)) for p, lane in everyone])
-    core_pair = send(
-        jnp.stack([own, across_chip]), [(place(p, lane), place(p, lane ^ 1)) for p, lane in everyone]
-    )
+    upper = jnp.where(upper_half, far, speed_class_map)
+    lower = jnp.where(upper_half, speed_class_map, far)
+    upper, spectral_entry_index, *crossing = lax.optimization_barrier(
+        (upper, spectral_entry_index, waves[2], waves[3])
+    )
+    across_chip = send(upper, in_plane(2))
+    starts += [send(v, shifted(r)) for r, v in zip((2, 3), crossing)]
+    lanes = jnp.stack([here, (plane - jnp.where(upper_half, 0, 1)) % planes]).astype(jnp.int32)
+    shape = jax.ShapeDtypeStruct
+    field = (2, columns // LANES, SUB * SUB, LANES)
+    half = pltpu.VMEM(field, jnp.float32)
+    natural = pltpu.VMEM((3,) + field[1:], jnp.float32)
+    turned = pltpu.VMEM((columns, LANES), jnp.float32)
+    block = pltpu.VMEM((LANES, columns), jnp.float32)
+    message = shape((3, rows, columns), jnp.float32)
+    field_bytes = 4 * 2 * SUB * SUB * columns
+
+    def folded_cells(kernel, *pieces):
+        return call(
+            kernel,
+            [shape((LEVELS,) + field[1:], jnp.int32)],
+            [pltpu.VMEM((LEVELS,) + field[1:], jnp.int32), block, turned],
+            (lanes, *pieces),
+            4 * field_bytes,
+        )[0]
 
     section = (plane - 1) % planes
     entry = spectral_entry_index[section, here]
@@ -449,62 +471,48 @@
     table = jnp.pad(table, ((0, 0), (0, 0), (0, LANES - NBIN)))
     table = jnp.broadcast_to(table[:, :, None, :], (ORDER + 1, 2, SUB, LANES))
 
-    owned = (plane - jnp.where(upper_half, 0, 1)) % planes
-    lanes = jnp.stack([here, owned]).astype(jnp.int32)
-    field = (2, columns // LANES, SUB * SUB, LANES)
-    natural = pltpu.VMEM((3,) + field[1:], jnp.float32)
-    half = pltpu.VMEM(field, jnp.float32)
-    turned = pltpu.VMEM((columns, LANES), jnp.float32)
-    block = pltpu.VMEM((LANES, columns), jnp.float32)
-    shape = jax.ShapeDtypeStruct
-    message = shape((3, rows, columns), jnp.float32)
-
-    (cells,) = call(
-        cells_kernel,
-        [shape((2 * LEVELS,) + field[1:], jnp.int32)],
-        [pltpu.VMEM((2 * LEVELS,) + field[1:], jnp.int32), block, turned],
-        lanes,
-        own,
-        across_chip,
-        core_pair,
-    )
+    core_pair = send(jnp.stack([upper, across_chip]), in_plane(1))
+    upper_cells = folded_cells(paired_cells_kernel, upper, across_chip, core_pair)
+    lower, upper_cells = lax.optimization_barrier((lower, upper_cells))
+    lower_pieces = [lower] + [send(lower, in_plane(r)) for r in (2, 1, 3)]
     bottom, *early = call(
         upper_kernel,
         [shape(field, jnp.float32)] + [message] * NFREQ,
         [half, half, half, block, turned, natural],
-        lanes,
-        *starts,
-        cells,
-        table,
-    )
+        (lanes, *starts, upper_cells, table),
+        80 * field_bytes,
+    )
+    early, lower_pieces = lax.optimization_barrier((early, lower_pieces))
     early = [
-        send(v, [(place(p, lane), place(p - (lane ^ r) // 2, lane ^ r)) for p, lane in everyone])
+        send(v, [(place(p, n), place(p - (n ^ r) // 2, n ^ r)) for p, n in everyone])
         for r, v in enumerate(early)
     ]
+    lower_cells = folded_cells(cells_kernel, *lower_pieces)
     late = call(
         lower_kernel,
         [message] * NFREQ,
         [half, half, half, half, natural],
-        lanes,
-        bottom,
-        cells,
-        table,
-    )
+        (lanes, bottom, lower_cells, table),
+        80 * field_bytes,
+    )
+    late, early = lax.optimization_barrier((late, early))
     late = [
-        send(v, [(place(p, lane), place(p + 1 - (lane ^ r) // 2, lane ^ r)) for p, lane in everyone])
+        send(v, [(place(p, n), place(p + 1 - (n ^ r) // 2, n ^ r)) for p, n in everyone])
         for r, v in enumerate(late)
     ]
-    handed, raw, squares = call(
-        final_kernel,
-        [
-            shape(incoming_wave.shape, jnp.float32),
-            shape(speed_class_map.shape, jnp.float32),
-            shape((SUB, LANES), jnp.float32),
-        ],
+    raw, squares = call(
+        image_kernel,
+        [shape(speed_class_map.shape, jnp.float32), shape((SUB, LANES), jnp.float32)],
+        [turned, block],
+        (lanes, *late, *early),
+        2 * field_bytes,
+    )
+    handed, raw = call(
+        handed_kernel,
+        [shape(incoming_wave.shape, jnp.float32), shape(speed_class_map.shape, jnp.float32)],
         [block, turned, block],
-        lanes,
-        *late,
-        *early,
+        (lanes, *late, *early, raw),
+        8 * field_bytes,
     )
 
     def owner(s, strip):

time: 88.3 us -> 77.6 us (0.88)
  waiting for transfers between devices: 30.5 us -> 17.5 us
  starting transfers between devices: 23.7 us -> 26.1 us
  Pallas kernels: 25 us -> 26.3 us
  local copies, waits for them, and re-layouts: 4.22 us -> 3.07 us
    ppermute x18 -> x21, waiting for transfers between devices: 30.5 us -> 17.5 us  [send(): return lax.ppermute(value, 'strip', pairs)]
    ppermute x18 -> x21, starting transfers between devices: 23.7 us -> 26.1 us  [send(): return lax.ppermute(value, 'strip', pairs)]
    pallas_call x4 -> x6, Pallas kernels: 25 us -> 26.3 us  [call(): pl.pallas_call(kernel, out_shape=outs, in_specs=[smem] + [vmem] * (len(op...]
    unnamed x8, local copies, waits for them, and re-layouts: 1.19 us -> 0.03 us
  transfers between devices with their start and end apart: 18 -> 21, of which waited for: 10 -> 9; matrix products, arithmetic and copies ran while one was open for 5% -> 5% of each run, Pallas kernels for 2% -> 33%
where the time goes in v1:
time: 77.6 us; the launch traced here: 77.4 us
  Pallas kernels  26.3 us (34%)
  starting transfers between devices  26.1 us (34%)
  waiting for transfers between devices  17.5 us (23%)
  local copies, waits for them, and re-layouts  3.07 us (4%)
  between operations  2.82 us (4%)
  other arithmetic  1.67 us (2%)
    pallas_call x6, Pallas kernels, call(): pl.pallas_call(kernel, out_shape=outs, in_specs=[smem] + [vmem] * (len(op...  26.3 us
    ppermute x21, starting transfers between devices, send(): return lax.ppermute(value, 'strip', pairs)  26.1 us
    ppermute x21, waiting for transfers between devices, send(): return lax.ppermute(value, 'strip', pairs)  17.5 us
  transfers between devices with their start and end apart: 21, of which 9 were waited for; matrix products, arithmetic and copies ran while one was open for 5% of the time, Pallas kernels for 33%

profile of v1, /device:TPU:0, one launch (start us, length us, event | category | flops | bytes accessed | tf_op | source)
XLA Modules:
  0.0 77.4 jit_solution(12296838470167242340)
XLA Ops:
  0.6 5.1 %collective-permute-start.2 = (s32[2,16,1024]{2,1,0:T(8,128)}, s32[2,16,1024]{2,1,0:T(8,128)S(1)}, u32[]{:S(2)}, u32[]{:S(2)}) collective-permute-start(s32[2,16,1024]{2,1,0:T(8,128)} %param.7), channel_id=1, source_target_pairs={{0,12},{1,13},{2,6},{3,7},{4,0},{5,1},{6,10},{7,11},{8,4},{9,5},{1... | collective-permute-start | bytes 393224 | tf_op jit(solution)/shard_map/ppermute | solution.py:420
  5.7 1.2 %dynamic-slice_bitcast_fusion = (f32[2,16,1024]{2,1,0:T(8,128)S(1)}, f32[2,16,1024]{2,1,0:T(8,128)S(1)}, f32[2,16,1024]{2,1,0:T(8,128)S(1)}, f32[2,16,1024]{2,1,0:T(8,128)S(1)}) fusion(f32[4,2,16,1024]{3,2,1,0:T(8,128)} %param.6, s32[]{:T(128)S(6)} %select_n.78, s32[]{:T(128)S(6)} %select_n.74, s32[]{:T(128)S(6)} %select_n.73, s32[]{:T(128)S(6)} %select_n.77), kind=kLoop, calls=%fused_computation.1 | loop fusion | bytes 1048592 | tf_op jit(solution)/shard_map/jit(dynamic_index_in_dim)/squeeze | solution.py:432
  6.9 0.7 collective-permute-start
  7.7 1.1 %collective-permute-done.2 = s32[2,16,1024]{2,1,0:T(8,128)S(1)} collective-permute-done((s32[2,16,1024]{2,1,0:T(8,128)}, s32[2,16,1024]{2,1,0:T(8,128)S(1)}, u32[]{:S(2)}, u32[]{:S(2)}) %collective-permute-start.2) | collective-permute-done | bytes 131104 | tf_op jit(solution)/shard_map/ppermute | solution.py:420
  8.8 2.2 %collective-permute-start.5 = (s32[2,16,1024]{2,1,0:T(8,128)S(1)}, s32[2,16,1024]{2,1,0:T(8,128)S(1)}, u32[]{:S(2)}, u32[]{:S(2)}) collective-permute-start(s32[2,16,1024]{2,1,0:T(8,128)S(1)} %get-tuple-element.39.own), channel_id=1, source_target_pairs={{0,2},{1,3},{2,0},{3,1},{4,6},{5,7},{6,4},{7,5},{8,10},{9,11},{10,... | collective-permute-start | bytes 393224 | tf_op jit(solution)/shard_map/ppermute | solution.py:420
  11.1 1.3 %dynamic_slice.27 = s32[1,1]{1,0:T(1,128)} dynamic-slice(s32[4,4]{1,0:T(4,128)} %param.8, s32[]{:T(128)S(6)} %select_n.81, s32[]{:T(128)S(6)} %select_n.73), dynamic_slice_sizes={1,1} | dynamic-slice | bytes 12 | tf_op jit(solution)/shard_map/dynamic_slice | solution.py:462
  13.8 1.3 %collective-permute-start.4 = (f32[2,16,1024]{2,1,0:T(8,128)S(1)}, f32[2,16,1024]{2,1,0:T(8,128)S(1)}, u32[]{:S(2)}, u32[]{:S(2)}) collective-permute-start(f32[2,16,1024]{2,1,0:T(8,128)S(1)} %get-tuple-element.38), channel_id=1, source_target_pairs={{0,3},{1,2},{2,5},{3,4},{4,7},{5,6},{6,9},{7,8},{8,11},{9,10},{10,... | collective-permute-start | bytes 393224 | tf_op jit(solution)/shard_map/ppermute | solution.py:420
  15.8 0.6 dynamic_slice.29
  16.5 0.8 %collective-permute-start.6 = (s32[2,2,16,1024]{3,2,1,0:T(8,128)S(1)}, s32[2,2,16,1024]{3,2,1,0:T(8,128)S(1)}, u32[]{:S(2)}, u32[]{:S(2)}) collective-permute-start(s32[2,2,16,1024]{3,2,1,0:T(8,128)S(1)} %pad_add_fusion), channel_id=1, source_target_pairs={{0,1},{1,0},{2,3},{3,2},{4,5},{5,4},{6,7},{7,6},{8,9},{9,8},{10,11... | collective-permute-start | bytes 786440 | tf_op jit(solution)/shard_map/ppermute | solution.py:420
  17.3 0.7 multiply_cosine_fusion
  18.0 0.4 collective-permute-done.6.pair
  18.5 1.0 %shard_map.77.cells = s32[2,8,64,128]{3,2,1,0:T(8,128)S(1)} custom-call(s32[2]{0:T(128)S(1)} %pad_add_fusion.1.lane_ref, s32[2,16,1024]{2,1,0:T(8,128)S(1)} %get-tuple-element.39.own, s32[2,16,1024]{2,1,0:T(8,128)S(1)} %collective-permute-done.5.two, s32[2,2,16,1024]{3,2,1,0:T(8,128)S(1)} %collective-permute-done.6.pair), custom_call_target="tpu_custom_call" | custom-call | flops 524288 | bytes 2097152 | tf_op jit(solution)/shard_map/pallas_call | solution.py:389
  20.0 1.7 %collective-permute-start.9 = (s32[2,16,1024]{2,1,0:T(8,128)S(1)}, s32[2,16,1024]{2,1,0:T(8,128)S(1)}, u32[]{:S(2)}, u32[]{:S(2)}) collective-permute-start(s32[2,16,1024]{2,1,0:T(8,128)S(1)} %get-tuple-element.48.own), channel_id=1, source_target_pairs={{0,3},{1,2},{2,1},{3,0},{4,7},{5,6},{6,5},{7,4},{8,11},{9,10},{10,... | collective-permute-start | bytes 393224 | tf_op jit(solution)/shard_map/ppermute | solution.py:420
  21.8 1.0 %collective-permute-done.3.w2 = f32[2,16,1024]{2,1,0:T(8,128)S(1)} collective-permute-done((f32[2,16,1024]{2,1,0:T(8,128)S(1)}, f32[2,16,1024]{2,1,0:T(8,128)S(1)}, u32[]{:S(2)}, u32[]{:S(2)}) %collective-permute-start.3) | collective-permute-done | bytes 131104 | tf_op jit(solution)/shard_map/ppermute | solution.py:420
  22.8 1.9 %collective-permute-done.4.w3 = f32[2,16,1024]{2,1,0:T(8,128)S(1)} collective-permute-done((f32[2,16,1024]{2,1,0:T(8,128)S(1)}, f32[2,16,1024]{2,1,0:T(8,128)S(1)}, u32[]{:S(2)}, u32[]{:S(2)}) %collective-permute-start.4) | collective-permute-done | bytes 131104 | tf_op jit(solution)/shard_map/ppermute | solution.py:420
  24.7 11.2 %shard_map.78 = (f32[2,8,64,128]{3,2,1,0:T(8,128)S(1)}, f32[3,16,1024]{2,1,0:T(8,128)S(1)}, f32[3,16,1024]{2,1,0:T(8,128)S(1)}, f32[3,16,1024]{2,1,0:T(8,128)S(1)}, f32[3,16,1024]{2,1,0:T(8,128)S(1)}) custom-call(s32[2]{0:T(128)S(1)} %pad_add_fusion.1.lane_ref, f32[2,16,1024]{2,1,0:T(8,128)S(1)} %collective-permute-done.w0, ...), custom_call_target="tpu_custom_call" | custom-call | flops 10485760 | bytes 41943040 | tf_op jit(solution)/shard_map/pallas_call | solution.py:389
  36.0 0.7 collective-permute-start.10
  37.0 3.0 %collective-permute-start.12 = (f32[3,16,1024]{2,1,0:T(8,128)S(1)}, f32[3,16,1024]{2,1,0:T(8,128)S(1)}, u32[]{:S(2)}, u32[]{:S(2)}) collective-permute-start(f32[3,16,1024]{2,1,0:T(8,128)S(1)} %get-tuple-element.58), channel_id=1, source_target_pairs={{0,14},{1,15},{2,0},{3,1},{4,2},{5,3},{6,4},{7,5},{8,6},{9,7},{10,... | collective-permute-start | bytes 589832 | tf_op jit(solution)/shard_map/ppermute | solution.py:420
  40.0 1.0 %shard_map.79.cells = s32[2,8,64,128]{3,2,1,0:T(8,128)S(1)} custom-call(s32[2]{0:T(128)S(1)} %pad_add_fusion.1.lane_ref, s32[2,16,1024]{2,1,0:T(8,128)S(1)} %get-tuple-element.48.own, s32[2,16,1024]{2,1,0:T(8,128)S(1)} %collective-permute-done.7.two, s32[2,16,1024]{2,1,0:T(8,128)S(1)} %collective-permute-done.8.one, ...), custom_call_target="tpu_custom_call" | custom-call | flops 524288 | bytes 2097152 | tf_op jit(solution)/shard_map/pallas_call | solution.py:389
  41.0 10.6 %shard_map.80 = (f32[3,16,1024]{2,1,0:T(8,128)S(1)}, f32[3,16,1024]{2,1,0:T(8,128)S(1)}, f32[3,16,1024]{2,1,0:T(8,128)S(1)}, f32[3,16,1024]{2,1,0:T(8,128)S(1)}) custom-call(s32[2]{0:T(128)S(1)} %pad_add_fusion.1.lane_ref, f32[2,8,64,128]{3,2,1,0:T(8,128)S(1)} %get-tuple-element.42.wave, s32[2,8,64,128]{3,2,1,0:T(8,128)S(1)} %shard_map.79.cells, ...), custom_call_target="tpu_custom_call" | custom-call | flops 10485760 | bytes 41943040 | tf_op jit(solution)/shard_map/pallas_call | solution.py:389
  51.7 3.6 %collective-permute-start.14 = (f32[3,16,1024]{2,1,0:T(8,128)S(1)}, f32[3,16,1024]{2,1,0:T(8,128)S(1)}, u32[]{:S(2)}, u32[]{:S(2)}) collective-permute-start(f32[3,16,1024]{2,1,0:T(8,128)S(1)} %get-tuple-element.60), channel_id=1, source_target_pairs={{0,4},{1,5},{2,2},{3,3},{4,8},{5,9},{6,6},{7,7},{8,12},{9,13},{10,... | collective-permute-start | bytes 589832 | tf_op jit(solution)/shard_map/ppermute | solution.py:420
  55.4 1.0 %collective-permute-start.17 = (f32[3,16,1024]{2,1,0:T(8,128)S(1)}, f32[3,16,1024]{2,1,0:T(8,128)S(1)}, u32[]{:S(2)}, u32[]{:S(2)}) collective-permute-start(f32[3,16,1024]{2,1,0:T(8,128)S(1)} %get-tuple-element.63), channel_id=1, source_target_pairs={{0,3},{1,2},{2,5},{3,4},{4,7},{5,6},{6,9},{7,8},{8,11},{9,10},{10,... | collective-permute-start | bytes 589832 | tf_op jit(solution)/shard_map/ppermute | solution.py:420
  56.4 6.7 %collective-permute-done.14.m0 = f32[3,16,1024]{2,1,0:T(8,128)S(1)} collective-permute-done((f32[3,16,1024]{2,1,0:T(8,128)S(1)}, f32[3,16,1024]{2,1,0:T(8,128)S(1)}, u32[]{:S(2)}, u32[]{:S(2)}) %collective-permute-start.14) | collective-permute-done | bytes 196640 | tf_op jit(solution)/shard_map/ppermute | solution.py:420
  63.1 2.7 %collective-permute-done.15.m1 = f32[3,16,1024]{2,1,0:T(8,128)S(1)} collective-permute-done((f32[3,16,1024]{2,1,0:T(8,128)S(1)}, f32[3,16,1024]{2,1,0:T(8,128)S(1)}, u32[]{:S(2)}, u32[]{:S(2)}) %collective-permute-start.15) | collective-permute-done | bytes 196640 | tf_op jit(solution)/shard_map/ppermute | solution.py:420
  65.8 2.7 %collective-permute-done.17.m3 = f32[3,16,1024]{2,1,0:T(8,128)S(1)} collective-permute-done((f32[3,16,1024]{2,1,0:T(8,128)S(1)}, f32[3,16,1024]{2,1,0:T(8,128)S(1)}, u32[]{:S(2)}, u32[]{:S(2)}) %collective-permute-start.17) | collective-permute-done | bytes 196640 | tf_op jit(solution)/shard_map/ppermute | solution.py:420
  68.5 0.7 shard_map.81
  69.3 0.6 collective-permute-start.18
  69.9 1.0 %collective-permute-start.19 = (f32[8,128]{1,0:T(8,128)S(1)}, f32[8,128]{1,0:T(8,128)S(1)}, u32[]{:S(2)}, u32[]{:S(2)}) collective-permute-start(f32[8,128]{1,0:T(8,128)S(1)} %get-tuple-element.70), channel_id=1, source_target_pairs={{2,4},{3,5},{4,2},{5,3},{6,8},{7,9},{8,6},{9,7},{10,12},{11,13},{1... | collective-permute-start | bytes 12296 | tf_op jit(solution)/shard_map/ppermute | solution.py:420
  70.9 3.1 %collective-permute-start.20 = (f32[8,128]{1,0:T(8,128)S(1)}, f32[8,128]{1,0:T(8,128)S(1)}, u32[]{:S(2)}, u32[]{:S(2)}) collective-permute-start(f32[8,128]{1,0:T(8,128)S(1)} %get-tuple-element.70), channel_id=1, source_target_pairs={{2,5},{3,4},{4,3},{5,2},{6,9},{7,8},{8,7},{9,6},{10,13},{11,12},{1... | collective-permute-start | bytes 12296 | tf_op jit(solution)/shard_map/ppermute | solution.py:420
  74.0 1.8 %shard_map.82 = (f32[4,2,16,1024]{3,2,1,0:T(8,128)}, f32[2,16,1024]{2,1,0:T(8,128)S(1)}) custom-call(s32[2]{0:T(128)S(1)} %pad_add_fusion.1.lane_ref, f32[3,16,1024]{2,1,0:T(8,128)S(1)} %collective-permute-done.14.m0, f32[3,16,1024]{2,1,0:T(8,128)S(1)} %collective-permute-done.15.m1, f32[3,16,1024]{2,1,0:T(8,128)S(1)} %collective-permute-done.16.m2, ...), custom_call_target="tpu_custom_call" | custom-call | flops 1048576 | bytes 4194304 | tf_op jit(solution)/shard_map/pallas_call | solution.py:389
  76.2 0.4 collective-permute-done.20
  76.6 0.7 broadcast_divide_fusion
  (40 shorter events, 1.9 us)
Async XLA Ops:
  0.6 17.4 %copy-start = (f32[16,16,2,13]{1,2,3,0:T(2,128)S(1)}, f32[16,16,2,13]{1,2,3,0:T(2,128)}, u32[]{:S(2)}) copy-start(f32[16,16,2,13]{1,2,3,0:T(2,128)} %param.9) | copy-start | bytes 79876
  0.6 8.2 %collective-permute-start.2 = (s32[2,16,1024]{2,1,0:T(8,128)}, s32[2,16,1024]{2,1,0:T(8,128)S(1)}, u32[]{:S(2)}, u32[]{:S(2)}) collective-permute-start(s32[2,16,1024]{2,1,0:T(8,128)} %param.7), channel_id=1, source_target_pairs={{0,12},{1,13},{2,6},{3,7},{4,0},{5,1},{6,10},{7,11},{8,4},{9,5},{1... | collective-permute-start | bytes 393224 | tf_op jit(solution)/shard_map/ppermute | solution.py:420
  5.7 3.1 %copy-start.1 = (s32[2,16,1024]{2,1,0:T(8,128)S(1)}, s32[2,16,1024]{2,1,0:T(8,128)}, u32[]{:S(2)}) copy-start(s32[2,16,1024]{2,1,0:T(8,128)} %param.7) | copy-start | bytes 393220
  6.9 12.9 %collective-permute-start = (f32[2,16,1024]{2,1,0:T(8,128)S(1)}, f32[2,16,1024]{2,1,0:T(8,128)S(1)}, u32[]{:S(2)}, u32[]{:S(2)}) collective-permute-start(f32[2,16,1024]{2,1,0:T(8,128)S(1)} %get-tuple-element.74), channel_id=1, source_target_pairs={{0,0},{1,1},{2,6},{3,7},{4,4},{5,5},{6,10},{7,11},{8,8},{9,9},{10,... | collective-permute-start | bytes 393224 | tf_op jit(solution)/shard_map/ppermute | solution.py:420
  7.6 12.4 %collective-permute-start.1 = (f32[2,16,1024]{2,1,0:T(8,128)S(1)}, f32[2,16,1024]{2,1,0:T(8,128)S(1)}, u32[]{:S(2)}, u32[]{:S(2)}) collective-permute-start(f32[2,16,1024]{2,1,0:T(8,128)S(1)} %get-tuple-element.73), channel_id=1, source_target_pairs={{0,1},{1,0},{2,7},{3,6},{4,5},{5,4},{6,11},{7,10},{8,9},{9,8},{10,... | collective-permute-start | bytes 393224 | tf_op jit(solution)/shard_map/ppermute | solution.py:420
  8.8 7.6 %collective-permute-start.5 = (s32[2,16,1024]{2,1,0:T(8,128)S(1)}, s32[2,16,1024]{2,1,0:T(8,128)S(1)}, u32[]{:S(2)}, u32[]{:S(2)}) collective-permute-start(s32[2,16,1024]{2,1,0:T(8,128)S(1)} %get-tuple-element.39.own), channel_id=1, source_target_pairs={{0,2},{1,3},{2,0},{3,1},{4,6},{5,7},{6,4},{7,5},{8,10},{9,11},{10,... | collective-permute-start | bytes 393224 | tf_op jit(solution)/shard_map/ppermute | solution.py:420
  13.7 2.1 %copy-start.3 = (f32[16]{0:T(128)S(1)}, f32[16]{0:T(128)}, u32[]{:S(2)}) copy-start(f32[16]{0:T(128)} %param.10) | copy-start | bytes 196
  13.7 9.1 %collective-permute-start.3 = (f32[2,16,1024]{2,1,0:T(8,128)S(1)}, f32[2,16,1024]{2,1,0:T(8,128)S(1)}, u32[]{:S(2)}, u32[]{:S(2)}) collective-permute-start(f32[2,16,1024]{2,1,0:T(8,128)S(1)} %get-tuple-element.37), channel_id=1, source_target_pairs={{0,2},{1,3},{2,4},{3,5},{4,6},{5,7},{6,8},{7,9},{8,10},{9,11},{10,... | collective-permute-start | bytes 393224 | tf_op jit(solution)/shard_map/ppermute | solution.py:420
  13.8 10.9 %collective-permute-start.4 = (f32[2,16,1024]{2,1,0:T(8,128)S(1)}, f32[2,16,1024]{2,1,0:T(8,128)S(1)}, u32[]{:S(2)}, u32[]{:S(2)}) collective-permute-start(f32[2,16,1024]{2,1,0:T(8,128)S(1)} %get-tuple-element.38), channel_id=1, source_target_pairs={{0,3},{1,2},{2,5},{3,4},{4,7},{5,6},{6,9},{7,8},{8,11},{9,10},{10,... | collective-permute-start | bytes 393224 | tf_op jit(solution)/shard_map/ppermute | solution.py:420
  16.5 0.9 %copy-start.2 = (f32[16]{0:T(128)S(1)}, f32[16]{0:T(128)}, u32[]{:S(2)}) copy-start(f32[16]{0:T(128)} %param.11) | copy-start | bytes 196
  16.5 2.0 %collective-permute-start.6 = (s32[2,2,16,1024]{3,2,1,0:T(8,128)S(1)}, s32[2,2,16,1024]{3,2,1,0:T(8,128)S(1)}, u32[]{:S(2)}, u32[]{:S(2)}) collective-permute-start(s32[2,2,16,1024]{3,2,1,0:T(8,128)S(1)} %pad_add_fusion), channel_id=1, source_target_pairs={{0,1},{1,0},{2,3},{3,2},{4,5},{5,4},{6,7},{7,6},{8,9},{9,8},{10,11... | collective-permute-start | bytes 786440 | tf_op jit(solution)/shard_map/ppermute | solution.py:420
  19.5 16.5 %collective-permute-start.7 = (s32[2,16,1024]{2,1,0:T(8,128)S(1)}, s32[2,16,1024]{2,1,0:T(8,128)S(1)}, u32[]{:S(2)}, u32[]{:S(2)}) collective-permute-start(s32[2,16,1024]{2,1,0:T(8,128)S(1)} %get-tuple-element.48.own), channel_id=1, source_target_pairs={{0,2},{1,3},{2,0},{3,1},{4,6},{5,7},{6,4},{7,5},{8,10},{9,11},{10,... | collective-permute-start | bytes 393224 | tf_op jit(solution)/shard_map/ppermute | solution.py:420
  19.8 16.1 %collective-permute-start.8 = (s32[2,16,1024]{2,1,0:T(8,128)S(1)}, s32[2,16,1024]{2,1,0:T(8,128)S(1)}, u32[]{:S(2)}, u32[]{:S(2)}) collective-permute-start(s32[2,16,1024]{2,1,0:T(8,128)S(1)} %get-tuple-element.48.own), channel_id=1, source_target_pairs={{0,1},{1,0},{2,3},{3,2},{4,5},{5,4},{6,7},{7,6},{8,9},{9,8},{10,11... | collective-permute-start | bytes 393224 | tf_op jit(solution)/shard_map/ppermute | solution.py:420
  20.0 16.0 %collective-permute-start.9 = (s32[2,16,1024]{2,1,0:T(8,128)S(1)}, s32[2,16,1024]{2,1,0:T(8,128)S(1)}, u32[]{:S(2)}, u32[]{:S(2)}) collective-permute-start(s32[2,16,1024]{2,1,0:T(8,128)S(1)} %get-tuple-element.48.own), channel_id=1, source_target_pairs={{0,3},{1,2},{2,1},{3,0},{4,7},{5,6},{6,5},{7,4},{8,11},{9,10},{10,... | collective-permute-start | bytes 393224 | tf_op jit(solution)/shard_map/ppermute | solution.py:420
  36.0 15.6 %collective-permute-start.10 = (f32[3,16,1024]{2,1,0:T(8,128)S(1)}, f32[3,16,1024]{2,1,0:T(8,128)S(1)}, u32[]{:S(2)}, u32[]{:S(2)}) collective-permute-start(f32[3,16,1024]{2,1,0:T(8,128)S(1)} %get-tuple-element.56), channel_id=1, source_target_pairs={{0,0},{1,1},{2,14},{3,15},{4,4},{5,5},{6,2},{7,3},{8,8},{9,9},{10,... | collective-permute-start | bytes 589832 | tf_op jit(solution)/shard_map/ppermute | solution.py:420
  36.7 15.0 %collective-permute-start.11 = (f32[3,16,1024]{2,1,0:T(8,128)S(1)}, f32[3,16,1024]{2,1,0:T(8,128)S(1)}, u32[]{:S(2)}, u32[]{:S(2)}) collective-permute-start(f32[3,16,1024]{2,1,0:T(8,128)S(1)} %get-tuple-element.57), channel_id=1, source_target_pairs={{0,1},{1,0},{2,15},{3,14},{4,5},{5,4},{6,3},{7,2},{8,9},{9,8},{10,... | collective-permute-start | bytes 589832 | tf_op jit(solution)/shard_map/ppermute | solution.py:420
  37.0 14.6 %collective-permute-start.12 = (f32[3,16,1024]{2,1,0:T(8,128)S(1)}, f32[3,16,1024]{2,1,0:T(8,128)S(1)}, u32[]{:S(2)}, u32[]{:S(2)}) collective-permute-start(f32[3,16,1024]{2,1,0:T(8,128)S(1)} %get-tuple-element.58), channel_id=1, source_target_pairs={{0,14},{1,15},{2,0},{3,1},{4,2},{5,3},{6,4},{7,5},{8,6},{9,7},{10,... | collective-permute-start | bytes 589832 | tf_op jit(solution)/shard_map/ppermute | solution.py:420
  40.0 11.6 %collective-permute-start.13 = (f32[3,16,1024]{2,1,0:T(8,128)S(1)}, f32[3,16,1024]{2,1,0:T(8,128)S(1)}, u32[]{:S(2)}, u32[]{:S(2)}) collective-permute-start(f32[3,16,1024]{2,1,0:T(8,128)S(1)} %get-tuple-element.59), channel_id=1, source_target_pairs={{0,15},{1,14},{2,1},{3,0},{4,3},{5,2},{6,5},{7,4},{8,7},{9,6},{10,... | collective-permute-start | bytes 589832 | tf_op jit(solution)/shard_map/ppermute | solution.py:420
  51.7 11.4 %collective-permute-start.14 = (f32[3,16,1024]{2,1,0:T(8,128)S(1)}, f32[3,16,1024]{2,1,0:T(8,128)S(1)}, u32[]{:S(2)}, u32[]{:S(2)}) collective-permute-start(f32[3,16,1024]{2,1,0:T(8,128)S(1)} %get-tuple-element.60), channel_id=1, source_target_pairs={{0,4},{1,5},{2,2},{3,3},{4,8},{5,9},{6,6},{7,7},{8,12},{9,13},{10,... | collective-permute-start | bytes 589832 | tf_op jit(solution)/shard_map/ppermute | solution.py:420
  55.3 10.5 %collective-permute-start.15 = (f32[3,16,1024]{2,1,0:T(8,128)S(1)}, f32[3,16,1024]{2,1,0:T(8,128)S(1)}, u32[]{:S(2)}, u32[]{:S(2)}) collective-permute-start(f32[3,16,1024]{2,1,0:T(8,128)S(1)} %get-tuple-element.61), channel_id=1, source_target_pairs={{0,5},{1,4},{2,3},{3,2},{4,9},{5,8},{6,7},{7,6},{8,13},{9,12},{10,... | collective-permute-start | bytes 589832 | tf_op jit(solution)/shard_map/ppermute | solution.py:420
  55.3 10.5 %collective-permute-start.16 = (f32[3,16,1024]{2,1,0:T(8,128)S(1)}, f32[3,16,1024]{2,1,0:T(8,128)S(1)}, u32[]{:S(2)}, u32[]{:S(2)}) collective-permute-start(f32[3,16,1024]{2,1,0:T(8,128)S(1)} %get-tuple-element.62), channel_id=1, source_target_pairs={{0,2},{1,3},{2,4},{3,5},{4,6},{5,7},{6,8},{7,9},{8,10},{9,11},{10,... | collective-permute-start | bytes 589832 | tf_op jit(solution)/shard_map/ppermute | solution.py:420
  55.4 13.1 %collective-permute-start.17 = (f32[3,16,1024]{2,1,0:T(8,128)S(1)}, f32[3,16,1024]{2,1,0:T(8,128)S(1)}, u32[]{:S(2)}, u32[]{:S(2)}) collective-permute-start(f32[3,16,1024]{2,1,0:T(8,128)S(1)} %get-tuple-element.63), channel_id=1, source_target_pairs={{0,3},{1,2},{2,5},{3,4},{4,7},{5,6},{6,9},{7,8},{8,11},{9,10},{10,... | collective-permute-start | bytes 589832 | tf_op jit(solution)/shard_map/ppermute | solution.py:420
  69.3 6.6 %collective-permute-start.18 = (f32[8,128]{1,0:T(8,128)S(1)}, f32[8,128]{1,0:T(8,128)S(1)}, u32[]{:S(2)}, u32[]{:S(2)}) collective-permute-start(f32[8,128]{1,0:T(8,128)S(1)} %get-tuple-element.70), channel_id=1, source_target_pairs={{2,3},{3,2},{4,5},{5,4},{6,7},{7,6},{8,9},{9,8},{10,11},{11,10},{1... | collective-permute-start | bytes 12296 | tf_op jit(solution)/shard_map/ppermute | solution.py:420
  69.9 6.3 %collective-permute-start.19 = (f32[8,128]{1,0:T(8,128)S(1)}, f32[8,128]{1,0:T(8,128)S(1)}, u32[]{:S(2)}, u32[]{:S(2)}) collective-permute-start(f32[8,128]{1,0:T(8,128)S(1)} %get-tuple-element.70), channel_id=1, source_target_pairs={{2,4},{3,5},{4,2},{5,3},{6,8},{7,9},{8,6},{9,7},{10,12},{11,13},{1... | collective-permute-start | bytes 12296 | tf_op jit(solution)/shard_map/ppermute | solution.py:420
  70.9 5.7 %collective-permute-start.20 = (f32[8,128]{1,0:T(8,128)S(1)}, f32[8,128]{1,0:T(8,128)S(1)}, u32[]{:S(2)}, u32[]{:S(2)}) collective-permute-start(f32[8,128]{1,0:T(8,128)S(1)} %get-tuple-element.70), channel_id=1, source_target_pairs={{2,5},{3,4},{4,3},{5,2},{6,9},{7,8},{8,7},{9,6},{10,13},{11,12},{1... | collective-permute-start | bytes 12296 | tf_op jit(solution)/shard_map/ppermute | solution.py:420

commit v2 on v1

--- a/solution.py
+++ b/solution.py
@@ -184,12 +184,26 @@
     return [q[j] + (q[j - 1] if j else before) for j in range(tiles)]
 
 
+def pick(table, index):
+    numbers = lax.GatherDimensionNumbers(
+        offset_dims=(),
+        collapsed_slice_dims=(1,),
+        start_index_map=(1,),
+        operand_batching_dims=(0,),
+        start_indices_batching_dims=(0,),
+    )
+    return lax.gather(
+        table,
+        index[..., None],
+        numbers,
+        slice_sizes=(1, 1),
+        mode=lax.GatherScatterMode.PROMISE_IN_BOUNDS,
+    )
+
+
 def weighted(table, cells, k, i, j):
-    index = cells[cell(i, j)]
-    return (
-        jnp.take_along_axis(table[k, 0], index, axis=1),
-        jnp.take_along_axis(table[k, 1], index, axis=1),
-    )
+    code = pick(table[k], cells[cell(i, j)])
+    return code.astype(jnp.float32), (code << 16).astype(jnp.float32)
 
 
 def advance(src, other, total, cells, table, k, tiles, first=False, mac=False):
@@ -233,7 +247,20 @@
                     total[im] = total[im] + b
 
 
-def one_level(src, even, odd, total, cells, table, tiles):
+def packed(table, codes, scale):
+    largest = jnp.zeros((SUB, LANES), jnp.float32)
+    for k in range(ORDER + 1):
+        for part in range(2):
+            largest = jnp.maximum(largest, jnp.abs(table[k, part]))
+    largest = jnp.where(largest > 0, largest, 1.0)
+    for k in range(ORDER + 1):
+        low = jnp.round(table[k, 1] / largest * 32767.0)
+        high = jnp.round(table[k, 0] / largest * 32767.0 - low / 65536.0)
+        codes[k] = high.astype(jnp.int32) * 65536 + low.astype(jnp.int32)
+    scale[...] = largest / (32767.0 * 65536.0)
+
+
+def one_level(src, even, odd, total, cells, table, scale, tiles):
     advance(src, odd, total, cells, table, 0, tiles, first=True, mac=True)
     for plane in range(2):
         for i in range(SUB):
@@ -253,8 +280,9 @@
             cr, ci = weighted(table, cells, ORDER, i, j)
             re, im = (0,) + cell(i, j), (1,) + cell(i, j)
             ur, ui = even[re], even[im]
-            total[re] = total[re] + (cr * ur - ci * ui)
-            total[im] = total[im] + (cr * ui + ci * ur)
+            unit = pick(scale[...], cells[cell(i, j)])
+            total[re] = (total[re] + (cr * ur - ci * ui)) * unit
+            total[im] = (total[im] + (cr * ui + ci * ur)) * unit
 
 
 def fold(block, turned, tiles):
@@ -310,7 +338,7 @@
 
 def upper_kernel(
     lane_ref, w0, w1, w2, w3, cells, table, bottom, o0, o1, o2, o3,
-    first, even, odd, block, turned, natural,
+    first, even, odd, block, turned, natural, codes, scale,
 ):
     here = lane_ref[0]
     rows = w0.shape[1]
@@ -329,16 +357,20 @@
     for j, tile in enumerate(fold(block, turned, tiles)):
         for plane in range(2):
             bottom[plane, j] = tile[64 * plane : 64 * plane + 64]
-    one_level(bottom, even, odd, first, cells.at[0], table, tiles)
-    one_level(first, even, odd, bottom, cells.at[1], table, tiles)
+    packed(table, codes, scale)
+    one_level(bottom, even, odd, first, cells.at[0], codes, scale, tiles)
+    one_level(first, even, odd, bottom, cells.at[1], codes, scale, tiles)
     rows_out(first, bottom, natural, (o0, o1, o2, o3), here, rows)
 
 
-def lower_kernel(lane_ref, wave, cells, table, o0, o1, o2, o3, first, second, even, odd, natural):
+def lower_kernel(
+    lane_ref, wave, cells, table, o0, o1, o2, o3, first, second, even, odd, natural, codes, scale
+):
     here = lane_ref[0]
     tiles = wave.shape[1]
-    one_level(wave, even, odd, first, cells.at[0], table, tiles)
-    one_level(first, even, odd, second, cells.at[1], table, tiles)
+    packed(table, codes, scale)
+    one_level(wave, even, odd, first, cells.at[0], codes, scale, tiles)
+    one_level(first, even, odd, second, cells.at[1], codes, scale, tiles)
     rows_out(first, second, natural, (o0, o1, o2, o3), here, o0.shape[1])
 
 
@@ -446,6 +478,8 @@
     natural = pltpu.VMEM((3,) + field[1:], jnp.float32)
     turned = pltpu.VMEM((columns, LANES), jnp.float32)
     block = pltpu.VMEM((LANES, columns), jnp.float32)
+    codes = pltpu.VMEM((ORDER + 1, SUB, LANES), jnp.int32)
+    scale = pltpu.VMEM((SUB, LANES), jnp.float32)
     message = shape((3, rows, columns), jnp.float32)
     field_bytes = 4 * 2 * SUB * SUB * columns
 
@@ -470,7 +504,6 @@
     table = jnp.stack([real, imag], axis=0).transpose(2, 0, 1)
     table = jnp.pad(table, ((0, 0), (0, 0), (0, LANES - NBIN)))
     table = jnp.broadcast_to(table[:, :, None, :], (ORDER + 1, 2, SUB, LANES))
-
     core_pair = send(jnp.stack([upper, across_chip]), in_plane(1))
     upper_cells = folded_cells(paired_cells_kernel, upper, across_chip, core_pair)
     lower, upper_cells = lax.optimization_barrier((lower, upper_cells))
@@ -478,7 +511,7 @@
     bottom, *early = call(
         upper_kernel,
         [shape(field, jnp.float32)] + [message] * NFREQ,
-        [half, half, half, block, turned, natural],
+        [half, half, half, block, turned, natural, codes, scale],
         (lanes, *starts, upper_cells, table),
         80 * field_bytes,
     )
@@ -491,7 +524,7 @@
     late = call(
         lower_kernel,
         [message] * NFREQ,
-        [half, half, half, half, natural],
+        [half, half, half, half, natural, codes, scale],
         (lanes, bottom, lower_cells, table),
         80 * field_bytes,
     )

time: 77.6 us -> 74 us (0.954)
  Pallas kernels: 26.3 us -> 22.6 us
    pallas_call x6, Pallas kernels: 26.3 us -> 22.6 us  [call(): pl.pallas_call(kernel, out_shape=outs, in_specs=[smem] + [vmem] * (len(op...]
  transfers between devices with their start and end apart: 21 -> 21, of which waited for: 9 -> 11; matrix products, arithmetic and copies ran while one was open for 5% -> 5% of each run, Pallas kernels for 33% -> 30%
where the time goes in v2:
time: 74 us; the launch traced here: 73.7 us
  starting transfers between devices  26 us (35%)
  Pallas kernels  22.6 us (31%)
  waiting for transfers between devices  17.6 us (24%)
  local copies, waits for them, and re-layouts  3.07 us (4%)
  between operations  2.82 us (4%)
  other arithmetic  1.67 us (2%)
    ppermute x21, starting transfers between devices, send(): return lax.ppermute(value, 'strip', pairs)  26 us
    pallas_call x6, Pallas kernels, call(): pl.pallas_call(kernel, out_shape=outs, in_specs=[smem] + [vmem] * (len(op...  22.6 us
    ppermute x21, waiting for transfers between devices, send(): return lax.ppermute(value, 'strip', pairs)  17.6 us
  transfers between devices with their start and end apart: 21, of which 11 were waited for; matrix products, arithmetic and copies ran while one was open for 5% of the time, Pallas kernels for 30%

profile of v2, /device:TPU:0, one launch (start us, length us, event | category | flops | bytes accessed | tf_op | source)
XLA Modules:
  0.0 73.7 jit_solution(5719882892416665546)
XLA Ops:
  0.6 5.1 %collective-permute-start.2 = (s32[2,16,1024]{2,1,0:T(8,128)}, s32[2,16,1024]{2,1,0:T(8,128)S(1)}, u32[]{:S(2)}, u32[]{:S(2)}) collective-permute-start(s32[2,16,1024]{2,1,0:T(8,128)} %param.7), channel_id=1, source_target_pairs={{0,12},{1,13},{2,6},{3,7},{4,0},{5,1},{6,10},{7,11},{8,4},{9,5},{1... | collective-permute-start | bytes 393224 | tf_op jit(solution)/shard_map/ppermute | solution.py:452
  5.7 1.2 %dynamic-slice_bitcast_fusion = (f32[2,16,1024]{2,1,0:T(8,128)S(1)}, f32[2,16,1024]{2,1,0:T(8,128)S(1)}, f32[2,16,1024]{2,1,0:T(8,128)S(1)}, f32[2,16,1024]{2,1,0:T(8,128)S(1)}) fusion(f32[4,2,16,1024]{3,2,1,0:T(8,128)} %param.6, s32[]{:T(128)S(6)} %select_n.78, s32[]{:T(128)S(6)} %select_n.74, s32[]{:T(128)S(6)} %select_n.73, s32[]{:T(128)S(6)} %select_n.77), kind=kLoop, calls=%fused_computation.1 | loop fusion | bytes 1048592 | tf_op jit(solution)/shard_map/jit(dynamic_index_in_dim)/squeeze | solution.py:464
  6.9 0.7 collective-permute-start
  7.7 1.1 %collective-permute-done.2 = s32[2,16,1024]{2,1,0:T(8,128)S(1)} collective-permute-done((s32[2,16,1024]{2,1,0:T(8,128)}, s32[2,16,1024]{2,1,0:T(8,128)S(1)}, u32[]{:S(2)}, u32[]{:S(2)}) %collective-permute-start.2) | collective-permute-done | bytes 131104 | tf_op jit(solution)/shard_map/ppermute | solution.py:452
  8.8 2.2 %collective-permute-start.5 = (s32[2,16,1024]{2,1,0:T(8,128)S(1)}, s32[2,16,1024]{2,1,0:T(8,128)S(1)}, u32[]{:S(2)}, u32[]{:S(2)}) collective-permute-start(s32[2,16,1024]{2,1,0:T(8,128)S(1)} %get-tuple-element.39.own), channel_id=1, source_target_pairs={{0,2},{1,3},{2,0},{3,1},{4,6},{5,7},{6,4},{7,5},{8,10},{9,11},{10,... | collective-permute-start | bytes 393224 | tf_op jit(solution)/shard_map/ppermute | solution.py:452
  11.1 1.3 %dynamic_slice.27 = s32[1,1]{1,0:T(1,128)} dynamic-slice(s32[4,4]{1,0:T(4,128)} %param.8, s32[]{:T(128)S(6)} %select_n.81, s32[]{:T(128)S(6)} %select_n.73), dynamic_slice_sizes={1,1} | dynamic-slice | bytes 12 | tf_op jit(solution)/shard_map/dynamic_slice | solution.py:496
  13.8 1.3 %collective-permute-start.4 = (f32[2,16,1024]{2,1,0:T(8,128)S(1)}, f32[2,16,1024]{2,1,0:T(8,128)S(1)}, u32[]{:S(2)}, u32[]{:S(2)}) collective-permute-start(f32[2,16,1024]{2,1,0:T(8,128)S(1)} %get-tuple-element.38), channel_id=1, source_target_pairs={{0,3},{1,2},{2,5},{3,4},{4,7},{5,6},{6,9},{7,8},{8,11},{9,10},{10,... | collective-permute-start | bytes 393224 | tf_op jit(solution)/shard_map/ppermute | solution.py:452
  15.8 0.6 dynamic_slice.29
  16.5 0.8 %collective-permute-start.6 = (s32[2,2,16,1024]{3,2,1,0:T(8,128)S(1)}, s32[2,2,16,1024]{3,2,1,0:T(8,128)S(1)}, u32[]{:S(2)}, u32[]{:S(2)}) collective-permute-start(s32[2,2,16,1024]{3,2,1,0:T(8,128)S(1)} %pad_add_fusion), channel_id=1, source_target_pairs={{0,1},{1,0},{2,3},{3,2},{4,5},{5,4},{6,7},{7,6},{8,9},{9,8},{10,11... | collective-permute-start | bytes 786440 | tf_op jit(solution)/shard_map/ppermute | solution.py:452
  17.3 0.7 multiply_cosine_fusion
  18.0 0.4 collective-permute-done.6.pair
  18.5 1.0 %shard_map.77.cells = s32[2,8,64,128]{3,2,1,0:T(8,128)S(1)} custom-call(s32[2]{0:T(128)S(1)} %pad_add_fusion.1.lane_ref, s32[2,16,1024]{2,1,0:T(8,128)S(1)} %get-tuple-element.39.own, s32[2,16,1024]{2,1,0:T(8,128)S(1)} %collective-permute-done.5.two, s32[2,2,16,1024]{3,2,1,0:T(8,128)S(1)} %collective-permute-done.6.pair), custom_call_target="tpu_custom_call" | custom-call | flops 524288 | bytes 2097152 | tf_op jit(solution)/shard_map/pallas_call | solution.py:421
  20.0 1.7 %collective-permute-start.9 = (s32[2,16,1024]{2,1,0:T(8,128)S(1)}, s32[2,16,1024]{2,1,0:T(8,128)S(1)}, u32[]{:S(2)}, u32[]{:S(2)}) collective-permute-start(s32[2,16,1024]{2,1,0:T(8,128)S(1)} %get-tuple-element.48.own), channel_id=1, source_target_pairs={{0,3},{1,2},{2,1},{3,0},{4,7},{5,6},{6,5},{7,4},{8,11},{9,10},{10,... | collective-permute-start | bytes 393224 | tf_op jit(solution)/shard_map/ppermute | solution.py:452
  21.8 1.0 %collective-permute-done.3.w2 = f32[2,16,1024]{2,1,0:T(8,128)S(1)} collective-permute-done((f32[2,16,1024]{2,1,0:T(8,128)S(1)}, f32[2,16,1024]{2,1,0:T(8,128)S(1)}, u32[]{:S(2)}, u32[]{:S(2)}) %collective-permute-start.3) | collective-permute-done | bytes 131104 | tf_op jit(solution)/shard_map/ppermute | solution.py:452
  22.8 1.9 %collective-permute-done.4.w3 = f32[2,16,1024]{2,1,0:T(8,128)S(1)} collective-permute-done((f32[2,16,1024]{2,1,0:T(8,128)S(1)}, f32[2,16,1024]{2,1,0:T(8,128)S(1)}, u32[]{:S(2)}, u32[]{:S(2)}) %collective-permute-start.4) | collective-permute-done | bytes 131104 | tf_op jit(solution)/shard_map/ppermute | solution.py:452
  24.7 9.4 %shard_map.78 = (f32[2,8,64,128]{3,2,1,0:T(8,128)S(1)}, f32[3,16,1024]{2,1,0:T(8,128)S(1)}, f32[3,16,1024]{2,1,0:T(8,128)S(1)}, f32[3,16,1024]{2,1,0:T(8,128)S(1)}, f32[3,16,1024]{2,1,0:T(8,128)S(1)}) custom-call(s32[2]{0:T(128)S(1)} %pad_add_fusion.1.lane_ref, f32[2,16,1024]{2,1,0:T(8,128)S(1)} %collective-permute-done.w0, ...), custom_call_target="tpu_custom_call" | custom-call | flops 10485760 | bytes 41943040 | tf_op jit(solution)/shard_map/pallas_call | solution.py:421
  34.2 0.7 collective-permute-start.10
  35.2 3.0 %collective-permute-start.12 = (f32[3,16,1024]{2,1,0:T(8,128)S(1)}, f32[3,16,1024]{2,1,0:T(8,128)S(1)}, u32[]{:S(2)}, u32[]{:S(2)}) collective-permute-start(f32[3,16,1024]{2,1,0:T(8,128)S(1)} %get-tuple-element.58), channel_id=1, source_target_pairs={{0,14},{1,15},{2,0},{3,1},{4,2},{5,3},{6,4},{7,5},{8,6},{9,7},{10,... | collective-permute-start | bytes 589832 | tf_op jit(solution)/shard_map/ppermute | solution.py:452
  38.2 1.0 %shard_map.79.cells = s32[2,8,64,128]{3,2,1,0:T(8,128)S(1)} custom-call(s32[2]{0:T(128)S(1)} %pad_add_fusion.1.lane_ref, s32[2,16,1024]{2,1,0:T(8,128)S(1)} %get-tuple-element.48.own, s32[2,16,1024]{2,1,0:T(8,128)S(1)} %collective-permute-done.7.two, s32[2,16,1024]{2,1,0:T(8,128)S(1)} %collective-permute-done.8.one, ...), custom_call_target="tpu_custom_call" | custom-call | flops 524288 | bytes 2097152 | tf_op jit(solution)/shard_map/pallas_call | solution.py:421
  39.2 8.7 %shard_map.80 = (f32[3,16,1024]{2,1,0:T(8,128)S(1)}, f32[3,16,1024]{2,1,0:T(8,128)S(1)}, f32[3,16,1024]{2,1,0:T(8,128)S(1)}, f32[3,16,1024]{2,1,0:T(8,128)S(1)}) custom-call(s32[2]{0:T(128)S(1)} %pad_add_fusion.1.lane_ref, f32[2,8,64,128]{3,2,1,0:T(8,128)S(1)} %get-tuple-element.42.wave, s32[2,8,64,128]{3,2,1,0:T(8,128)S(1)} %shard_map.79.cells, ...), custom_call_target="tpu_custom_call" | custom-call | flops 10485760 | bytes 41943040 | tf_op jit(solution)/shard_map/pallas_call | solution.py:421
  48.1 3.5 %collective-permute-start.14 = (f32[3,16,1024]{2,1,0:T(8,128)S(1)}, f32[3,16,1024]{2,1,0:T(8,128)S(1)}, u32[]{:S(2)}, u32[]{:S(2)}) collective-permute-start(f32[3,16,1024]{2,1,0:T(8,128)S(1)} %get-tuple-element.60), channel_id=1, source_target_pairs={{0,4},{1,5},{2,2},{3,3},{4,8},{5,9},{6,6},{7,7},{8,12},{9,13},{10,... | collective-permute-start | bytes 589832 | tf_op jit(solution)/shard_map/ppermute | solution.py:452
  51.8 1.0 %collective-permute-start.17 = (f32[3,16,1024]{2,1,0:T(8,128)S(1)}, f32[3,16,1024]{2,1,0:T(8,128)S(1)}, u32[]{:S(2)}, u32[]{:S(2)}) collective-permute-start(f32[3,16,1024]{2,1,0:T(8,128)S(1)} %get-tuple-element.63), channel_id=1, source_target_pairs={{0,3},{1,2},{2,5},{3,4},{4,7},{5,6},{6,9},{7,8},{8,11},{9,10},{10,... | collective-permute-start | bytes 589832 | tf_op jit(solution)/shard_map/ppermute | solution.py:452
  52.7 6.8 %collective-permute-done.14.m0 = f32[3,16,1024]{2,1,0:T(8,128)S(1)} collective-permute-done((f32[3,16,1024]{2,1,0:T(8,128)S(1)}, f32[3,16,1024]{2,1,0:T(8,128)S(1)}, u32[]{:S(2)}, u32[]{:S(2)}) %collective-permute-start.14) | collective-permute-done | bytes 196640 | tf_op jit(solution)/shard_map/ppermute | solution.py:452
  59.5 2.6 %collective-permute-done.15.m1 = f32[3,16,1024]{2,1,0:T(8,128)S(1)} collective-permute-done((f32[3,16,1024]{2,1,0:T(8,128)S(1)}, f32[3,16,1024]{2,1,0:T(8,128)S(1)}, u32[]{:S(2)}, u32[]{:S(2)}) %collective-permute-start.15) | collective-permute-done | bytes 196640 | tf_op jit(solution)/shard_map/ppermute | solution.py:452
  62.2 2.7 %collective-permute-done.17.m3 = f32[3,16,1024]{2,1,0:T(8,128)S(1)} collective-permute-done((f32[3,16,1024]{2,1,0:T(8,128)S(1)}, f32[3,16,1024]{2,1,0:T(8,128)S(1)}, u32[]{:S(2)}, u32[]{:S(2)}) %collective-permute-start.17) | collective-permute-done | bytes 196640 | tf_op jit(solution)/shard_map/ppermute | solution.py:452
  64.9 0.7 shard_map.81
  65.6 0.6 collective-permute-start.18
  66.3 1.0 %collective-permute-start.19 = (f32[8,128]{1,0:T(8,128)S(1)}, f32[8,128]{1,0:T(8,128)S(1)}, u32[]{:S(2)}, u32[]{:S(2)}) collective-permute-start(f32[8,128]{1,0:T(8,128)S(1)} %get-tuple-element.70), channel_id=1, source_target_pairs={{2,4},{3,5},{4,2},{5,3},{6,8},{7,9},{8,6},{9,7},{10,12},{11,13},{1... | collective-permute-start | bytes 12296 | tf_op jit(solution)/shard_map/ppermute | solution.py:452
  67.3 3.1 %collective-permute-start.20 = (f32[8,128]{1,0:T(8,128)S(1)}, f32[8,128]{1,0:T(8,128)S(1)}, u32[]{:S(2)}, u32[]{:S(2)}) collective-permute-start(f32[8,128]{1,0:T(8,128)S(1)} %get-tuple-element.70), channel_id=1, source_target_pairs={{2,5},{3,4},{4,3},{5,2},{6,9},{7,8},{8,7},{9,6},{10,13},{11,12},{1... | collective-permute-start | bytes 12296 | tf_op jit(solution)/shard_map/ppermute | solution.py:452
  70.4 1.8 %shard_map.82 = (f32[4,2,16,1024]{3,2,1,0:T(8,128)}, f32[2,16,1024]{2,1,0:T(8,128)S(1)}) custom-call(s32[2]{0:T(128)S(1)} %pad_add_fusion.1.lane_ref, f32[3,16,1024]{2,1,0:T(8,128)S(1)} %collective-permute-done.14.m0, f32[3,16,1024]{2,1,0:T(8,128)S(1)} %collective-permute-done.15.m1, f32[3,16,1024]{2,1,0:T(8,128)S(1)} %collective-permute-done.16.m2, ...), custom_call_target="tpu_custom_call" | custom-call | flops 1048576 | bytes 4194304 | tf_op jit(solution)/shard_map/pallas_call | solution.py:421
  72.6 0.4 collective-permute-done.20
  73.0 0.7 %broadcast_divide_fusion = f32[2,16,1024]{2,1,0:T(8,128)} fusion(f32[2,16,1024]{2,1,0:T(8,128)S(1)} %get-tuple-element.69, f32[2]{0:T(128)S(1)} %sqrt_bitcast_fusion), kind=kLoop, calls=%fused_computation.5 | loop fusion | flops 32768 | bytes 262152 | tf_op jit(solution)/shard_map/div | solution.py:561
  (40 shorter events, 2.1 us)
Async XLA Ops:
  0.6 17.4 %copy-start = (f32[16,16,2,13]{1,2,3,0:T(2,128)S(1)}, f32[16,16,2,13]{1,2,3,0:T(2,128)}, u32[]{:S(2)}) copy-start(f32[16,16,2,13]{1,2,3,0:T(2,128)} %param.9) | copy-start | bytes 79876
  0.6 8.2 %collective-permute-start.2 = (s32[2,16,1024]{2,1,0:T(8,128)}, s32[2,16,1024]{2,1,0:T(8,128)S(1)}, u32[]{:S(2)}, u32[]{:S(2)}) collective-permute-start(s32[2,16,1024]{2,1,0:T(8,128)} %param.7), channel_id=1, source_target_pairs={{0,12},{1,13},{2,6},{3,7},{4,0},{5,1},{6,10},{7,11},{8,4},{9,5},{1... | collective-permute-start | bytes 393224 | tf_op jit(solution)/shard_map/ppermute | solution.py:452
  5.7 3.1 %copy-start.1 = (s32[2,16,1024]{2,1,0:T(8,128)S(1)}, s32[2,16,1024]{2,1,0:T(8,128)}, u32[]{:S(2)}) copy-start(s32[2,16,1024]{2,1,0:T(8,128)} %param.7) | copy-start | bytes 393220
  6.9 12.9 %collective-permute-start = (f32[2,16,1024]{2,1,0:T(8,128)S(1)}, f32[2,16,1024]{2,1,0:T(8,128)S(1)}, u32[]{:S(2)}, u32[]{:S(2)}) collective-permute-start(f32[2,16,1024]{2,1,0:T(8,128)S(1)} %get-tuple-element.74), channel_id=1, source_target_pairs={{0,0},{1,1},{2,6},{3,7},{4,4},{5,5},{6,10},{7,11},{8,8},{9,9},{10,... | collective-permute-start | bytes 393224 | tf_op jit(solution)/shard_map/ppermute | solution.py:452
  7.6 12.4 %collective-permute-start.1 = (f32[2,16,1024]{2,1,0:T(8,128)S(1)}, f32[2,16,1024]{2,1,0:T(8,128)S(1)}, u32[]{:S(2)}, u32[]{:S(2)}) collective-permute-start(f32[2,16,1024]{2,1,0:T(8,128)S(1)} %get-tuple-element.73), channel_id=1, source_target_pairs={{0,1},{1,0},{2,7},{3,6},{4,5},{5,4},{6,11},{7,10},{8,9},{9,8},{10,... | collective-permute-start | bytes 393224 | tf_op jit(solution)/shard_map/ppermute | solution.py:452
  8.8 7.6 %collective-permute-start.5 = (s32[2,16,1024]{2,1,0:T(8,128)S(1)}, s32[2,16,1024]{2,1,0:T(8,128)S(1)}, u32[]{:S(2)}, u32[]{:S(2)}) collective-permute-start(s32[2,16,1024]{2,1,0:T(8,128)S(1)} %get-tuple-element.39.own), channel_id=1, source_target_pairs={{0,2},{1,3},{2,0},{3,1},{4,6},{5,7},{6,4},{7,5},{8,10},{9,11},{10,... | collective-permute-start | bytes 393224 | tf_op jit(solution)/shard_map/ppermute | solution.py:452
  13.7 2.1 %copy-start.3 = (f32[16]{0:T(128)S(1)}, f32[16]{0:T(128)}, u32[]{:S(2)}) copy-start(f32[16]{0:T(128)} %param.10) | copy-start | bytes 196
  13.7 9.1 %collective-permute-start.3 = (f32[2,16,1024]{2,1,0:T(8,128)S(1)}, f32[2,16,1024]{2,1,0:T(8,128)S(1)}, u32[]{:S(2)}, u32[]{:S(2)}) collective-permute-start(f32[2,16,1024]{2,1,0:T(8,128)S(1)} %get-tuple-element.37), channel_id=1, source_target_pairs={{0,2},{1,3},{2,4},{3,5},{4,6},{5,7},{6,8},{7,9},{8,10},{9,11},{10,... | collective-permute-start | bytes 393224 | tf_op jit(solution)/shard_map/ppermute | solution.py:452
  13.8 10.9 %collective-permute-start.4 = (f32[2,16,1024]{2,1,0:T(8,128)S(1)}, f32[2,16,1024]{2,1,0:T(8,128)S(1)}, u32[]{:S(2)}, u32[]{:S(2)}) collective-permute-start(f32[2,16,1024]{2,1,0:T(8,128)S(1)} %get-tuple-element.38), channel_id=1, source_target_pairs={{0,3},{1,2},{2,5},{3,4},{4,7},{5,6},{6,9},{7,8},{8,11},{9,10},{10,... | collective-permute-start | bytes 393224 | tf_op jit(solution)/shard_map/ppermute | solution.py:452
  16.5 0.9 %copy-start.2 = (f32[16]{0:T(128)S(1)}, f32[16]{0:T(128)}, u32[]{:S(2)}) copy-start(f32[16]{0:T(128)} %param.11) | copy-start | bytes 196
  16.5 2.0 %collective-permute-start.6 = (s32[2,2,16,1024]{3,2,1,0:T(8,128)S(1)}, s32[2,2,16,1024]{3,2,1,0:T(8,128)S(1)}, u32[]{:S(2)}, u32[]{:S(2)}) collective-permute-start(s32[2,2,16,1024]{3,2,1,0:T(8,128)S(1)} %pad_add_fusion), channel_id=1, source_target_pairs={{0,1},{1,0},{2,3},{3,2},{4,5},{5,4},{6,7},{7,6},{8,9},{9,8},{10,11... | collective-permute-start | bytes 786440 | tf_op jit(solution)/shard_map/ppermute | solution.py:452
  19.5 14.7 %collective-permute-start.7 = (s32[2,16,1024]{2,1,0:T(8,128)S(1)}, s32[2,16,1024]{2,1,0:T(8,128)S(1)}, u32[]{:S(2)}, u32[]{:S(2)}) collective-permute-start(s32[2,16,1024]{2,1,0:T(8,128)S(1)} %get-tuple-element.48.own), channel_id=1, source_target_pairs={{0,2},{1,3},{2,0},{3,1},{4,6},{5,7},{6,4},{7,5},{8,10},{9,11},{10,... | collective-permute-start | bytes 393224 | tf_op jit(solution)/shard_map/ppermute | solution.py:452
  19.8 14.3 %collective-permute-start.8 = (s32[2,16,1024]{2,1,0:T(8,128)S(1)}, s32[2,16,1024]{2,1,0:T(8,128)S(1)}, u32[]{:S(2)}, u32[]{:S(2)}) collective-permute-start(s32[2,16,1024]{2,1,0:T(8,128)S(1)} %get-tuple-element.48.own), channel_id=1, source_target_pairs={{0,1},{1,0},{2,3},{3,2},{4,5},{5,4},{6,7},{7,6},{8,9},{9,8},{10,11... | collective-permute-start | bytes 393224 | tf_op jit(solution)/shard_map/ppermute | solution.py:452
  20.0 14.2 %collective-permute-start.9 = (s32[2,16,1024]{2,1,0:T(8,128)S(1)}, s32[2,16,1024]{2,1,0:T(8,128)S(1)}, u32[]{:S(2)}, u32[]{:S(2)}) collective-permute-start(s32[2,16,1024]{2,1,0:T(8,128)S(1)} %get-tuple-element.48.own), channel_id=1, source_target_pairs={{0,3},{1,2},{2,1},{3,0},{4,7},{5,6},{6,5},{7,4},{8,11},{9,10},{10,... | collective-permute-start | bytes 393224 | tf_op jit(solution)/shard_map/ppermute | solution.py:452
  34.2 13.8 %collective-permute-start.10 = (f32[3,16,1024]{2,1,0:T(8,128)S(1)}, f32[3,16,1024]{2,1,0:T(8,128)S(1)}, u32[]{:S(2)}, u32[]{:S(2)}) collective-permute-start(f32[3,16,1024]{2,1,0:T(8,128)S(1)} %get-tuple-element.56), channel_id=1, source_target_pairs={{0,0},{1,1},{2,14},{3,15},{4,4},{5,5},{6,2},{7,3},{8,8},{9,9},{10,... | collective-permute-start | bytes 589832 | tf_op jit(solution)/shard_map/ppermute | solution.py:452
  34.8 13.1 %collective-permute-start.11 = (f32[3,16,1024]{2,1,0:T(8,128)S(1)}, f32[3,16,1024]{2,1,0:T(8,128)S(1)}, u32[]{:S(2)}, u32[]{:S(2)}) collective-permute-start(f32[3,16,1024]{2,1,0:T(8,128)S(1)} %get-tuple-element.57), channel_id=1, source_target_pairs={{0,1},{1,0},{2,15},{3,14},{4,5},{5,4},{6,3},{7,2},{8,9},{9,8},{10,... | collective-permute-start | bytes 589832 | tf_op jit(solution)/shard_map/ppermute | solution.py:452
  35.2 12.8 %collective-permute-start.12 = (f32[3,16,1024]{2,1,0:T(8,128)S(1)}, f32[3,16,1024]{2,1,0:T(8,128)S(1)}, u32[]{:S(2)}, u32[]{:S(2)}) collective-permute-start(f32[3,16,1024]{2,1,0:T(8,128)S(1)} %get-tuple-element.58), channel_id=1, source_target_pairs={{0,14},{1,15},{2,0},{3,1},{4,2},{5,3},{6,4},{7,5},{8,6},{9,7},{10,... | collective-permute-start | bytes 589832 | tf_op jit(solution)/shard_map/ppermute | solution.py:452
  38.2 9.9 %collective-permute-start.13 = (f32[3,16,1024]{2,1,0:T(8,128)S(1)}, f32[3,16,1024]{2,1,0:T(8,128)S(1)}, u32[]{:S(2)}, u32[]{:S(2)}) collective-permute-start(f32[3,16,1024]{2,1,0:T(8,128)S(1)} %get-tuple-element.59), channel_id=1, source_target_pairs={{0,15},{1,14},{2,1},{3,0},{4,3},{5,2},{6,5},{7,4},{8,7},{9,6},{10,... | collective-permute-start | bytes 589832 | tf_op jit(solution)/shard_map/ppermute | solution.py:452
  48.1 11.4 %collective-permute-start.14 = (f32[3,16,1024]{2,1,0:T(8,128)S(1)}, f32[3,16,1024]{2,1,0:T(8,128)S(1)}, u32[]{:S(2)}, u32[]{:S(2)}) collective-permute-start(f32[3,16,1024]{2,1,0:T(8,128)S(1)} %get-tuple-element.60), channel_id=1, source_target_pairs={{0,4},{1,5},{2,2},{3,3},{4,8},{5,9},{6,6},{7,7},{8,12},{9,13},{10,... | collective-permute-start | bytes 589832 | tf_op jit(solution)/shard_map/ppermute | solution.py:452
  51.6 10.4 %collective-permute-start.15 = (f32[3,16,1024]{2,1,0:T(8,128)S(1)}, f32[3,16,1024]{2,1,0:T(8,128)S(1)}, u32[]{:S(2)}, u32[]{:S(2)}) collective-permute-start(f32[3,16,1024]{2,1,0:T(8,128)S(1)} %get-tuple-element.61), channel_id=1, source_target_pairs={{0,5},{1,4},{2,3},{3,2},{4,9},{5,8},{6,7},{7,6},{8,13},{9,12},{10,... | collective-permute-start | bytes 589832 | tf_op jit(solution)/shard_map/ppermute | solution.py:452
  51.7 10.5 %collective-permute-start.16 = (f32[3,16,1024]{2,1,0:T(8,128)S(1)}, f32[3,16,1024]{2,1,0:T(8,128)S(1)}, u32[]{:S(2)}, u32[]{:S(2)}) collective-permute-start(f32[3,16,1024]{2,1,0:T(8,128)S(1)} %get-tuple-element.62), channel_id=1, source_target_pairs={{0,2},{1,3},{2,4},{3,5},{4,6},{5,7},{6,8},{7,9},{8,10},{9,11},{10,... | collective-permute-start | bytes 589832 | tf_op jit(solution)/shard_map/ppermute | solution.py:452
  51.8 13.1 %collective-permute-start.17 = (f32[3,16,1024]{2,1,0:T(8,128)S(1)}, f32[3,16,1024]{2,1,0:T(8,128)S(1)}, u32[]{:S(2)}, u32[]{:S(2)}) collective-permute-start(f32[3,16,1024]{2,1,0:T(8,128)S(1)} %get-tuple-element.63), channel_id=1, source_target_pairs={{0,3},{1,2},{2,5},{3,4},{4,7},{5,6},{6,9},{7,8},{8,11},{9,10},{10,... | collective-permute-start | bytes 589832 | tf_op jit(solution)/shard_map/ppermute | solution.py:452
  65.6 6.6 %collective-permute-start.18 = (f32[8,128]{1,0:T(8,128)S(1)}, f32[8,128]{1,0:T(8,128)S(1)}, u32[]{:S(2)}, u32[]{:S(2)}) collective-permute-start(f32[8,128]{1,0:T(8,128)S(1)} %get-tuple-element.70), channel_id=1, source_target_pairs={{2,3},{3,2},{4,5},{5,4},{6,7},{7,6},{8,9},{9,8},{10,11},{11,10},{1... | collective-permute-start | bytes 12296 | tf_op jit(solution)/shard_map/ppermute | solution.py:452
  66.3 6.3 %collective-permute-start.19 = (f32[8,128]{1,0:T(8,128)S(1)}, f32[8,128]{1,0:T(8,128)S(1)}, u32[]{:S(2)}, u32[]{:S(2)}) collective-permute-start(f32[8,128]{1,0:T(8,128)S(1)} %get-tuple-element.70), channel_id=1, source_target_pairs={{2,4},{3,5},{4,2},{5,3},{6,8},{7,9},{8,6},{9,7},{10,12},{11,13},{1... | collective-permute-start | bytes 12296 | tf_op jit(solution)/shard_map/ppermute | solution.py:452
  67.3 5.7 %collective-permute-start.20 = (f32[8,128]{1,0:T(8,128)S(1)}, f32[8,128]{1,0:T(8,128)S(1)}, u32[]{:S(2)}, u32[]{:S(2)}) collective-permute-start(f32[8,128]{1,0:T(8,128)S(1)} %get-tuple-element.70), channel_id=1, source_target_pairs={{2,5},{3,4},{4,3},{5,2},{6,9},{7,8},{8,7},{9,6},{10,13},{11,12},{1... | collective-permute-start | bytes 12296 | tf_op jit(solution)/shard_map/ppermute | solution.py:452

commit v3 on v2

--- a/solution.py
+++ b/solution.py
@@ -206,12 +206,11 @@
     return code.astype(jnp.float32), (code << 16).astype(jnp.float32)
 
 
-def advance(src, other, total, cells, table, k, tiles, first=False, mac=False):
+def advance(src, other, tiles, first=False):
     edges = [rim(src, plane, tiles) for plane in range(2)]
     above = [e[1] for e in edges]
     present = [e[2] for e in edges]
     for i in range(SUB):
-        new, old = [], []
         for plane in range(2):
             if i < SUB - 1:
                 below = [src[(plane,) + cell(i + 1, j)] for j in range(tiles)]
@@ -221,30 +220,29 @@
                 pairs = edges[plane][0]
             h = across([pairs[j] + above[plane][j] for j in range(tiles)])
             above[plane] = pairs
-            out = []
             for j in range(tiles):
                 at = (plane,) + cell(i, j)
                 v = present[plane][j]
                 u = v - 0.125 * h[j] if first else (v + v) - (0.25 * h[j] + other[at])
                 other[at] = u
-                out.append(u)
-            old.append(present[plane])
             present[plane] = below
-            new.append(out)
-        if mac:
-            for j in range(tiles):
-                c0r, c0i = weighted(table, cells, k, i, j)
-                c1r, c1i = weighted(table, cells, k + 1, i, j)
-                ur, ui = new[0][j], new[1][j]
-                vr, vi = old[0][j], old[1][j]
-                a = (c1r * ur - c1i * ui) + (c0r * vr - c0i * vi)
-                b = (c1r * ui + c1i * ur) + (c0r * vi + c0i * vr)
-                re, im = (0,) + cell(i, j), (1,) + cell(i, j)
-                if first:
-                    total[re], total[im] = a, b
-                else:
-                    total[re] = total[re] + a
-                    total[im] = total[im] + b
+
+
+def add_orders(lower, upper, total, cells, table, k, tiles, first=False):
+    for i in range(SUB):
+        for j in range(tiles):
+            c0r, c0i = weighted(table, cells, k, i, j)
+            c1r, c1i = weighted(table, cells, k + 1, i, j)
+            re, im = (0,) + cell(i, j), (1,) + cell(i, j)
+            ur, ui = upper[re], upper[im]
+            vr, vi = lower[re], lower[im]
+            a = (c1r * ur - c1i * ui) + (c0r * vr - c0i * vi)
+            b = (c1r * ui + c1i * ur) + (c0r * vi + c0i * vr)
+            if first:
+                total[re], total[im] = a, b
+            else:
+                total[re] = total[re] + a
+                total[im] = total[im] + b
 
 
 def packed(table, codes, scale):
@@ -261,7 +259,8 @@
 
 
 def one_level(src, even, odd, total, cells, table, scale, tiles):
-    advance(src, odd, total, cells, table, 0, tiles, first=True, mac=True)
+    advance(src, odd, tiles, first=True)
+    add_orders(src, odd, total, cells, table, 0, tiles, first=True)
     for plane in range(2):
         for i in range(SUB):
             for j in range(tiles):
@@ -269,12 +268,13 @@
 
     def pair(t, carry):
         k = 2 * t + 1
-        advance(odd, even, total, cells, table, k, tiles)
-        advance(even, odd, total, cells, table, k + 1, tiles, mac=True)
+        advance(odd, even, tiles)
+        advance(even, odd, tiles)
+        add_orders(even, odd, total, cells, table, k + 1, tiles)
         return carry
 
     lax.fori_loop(0, ORDER // 2 - 1, pair, 0)
-    advance(odd, even, total, cells, table, ORDER - 1, tiles)
+    advance(odd, even, tiles)
     for i in range(SUB):
         for j in range(tiles):
             cr, ci = weighted(table, cells, ORDER, i, j)
@@ -415,6 +415,13 @@
             image[level, :, column(j)] = tile[rows * level : rows * level + rows]
 
 
+def scale_kernel(cells_ref, raw, s0, s1, s2, s3, image):
+    mean = ((s0[...] + s1[...]) + (s2[...] + s3[...])) / cells_ref[0].astype(jnp.float32)
+    root = jnp.sqrt(mean + 1e-06)
+    for level in range(LEVELS):
+        image[level] = raw[level] / root[0:1, level : level + 1]
+
+
 def call(kernel, outs, scratch, operands, moved=0):
     vmem = pl.BlockSpec(memory_space=pltpu.VMEM)
     smem = pl.BlockSpec(memory_space=pltpu.SMEM)
@@ -551,14 +558,17 @@
     def owner(s, strip):
         return place(s + strip // 2, strip ^ 2)
 
-    mean_square = squares
-    for r in range(1, NFREQ):
-        mean_square = mean_square + send(
+    sums = [squares] + [
+        send(
             squares,
             [(owner(s, strip), owner(s, strip ^ r)) for s in range(planes) for strip in range(NFREQ)],
         )
-    mean_square = mean_square[0, :LEVELS] / (rows * NFREQ * columns)
-    image = raw / jnp.sqrt(mean_square + 1e-06)[:, None, None]
+        for r in range(1, NFREQ)
+    ]
+    section_cells = jnp.full((1,), rows * NFREQ * columns, jnp.int32)
+    (image,) = call(
+        scale_kernel, [shape(raw.shape, jnp.float32)], [], (section_cells, raw, *sums), field_bytes
+    )
     return (image, handed)
 
 

time: 74 us -> 72.2 us (0.976)
  Pallas kernels: 22.6 us -> 21.5 us
  starting transfers between devices: 26 us -> 25.2 us
  waiting for transfers between devices: 17.6 us -> 18.4 us
  other arithmetic: 1.67 us -> 0.91 us
    pallas_call x6 -> x7, Pallas kernels: 22.6 us -> 21.5 us  [call(): pl.pallas_call(kernel, out_shape=outs, in_specs=[smem] + [vmem] * (len(op...]
    ppermute x21, waiting for transfers between devices: 17.6 us -> 18.4 us  [send(): return lax.ppermute(value, 'strip', pairs)]
    ppermute x21, starting transfers between devices: 26 us -> 25.2 us  [send(): return lax.ppermute(value, 'strip', pairs)]
    div x1 -> x0, other arithmetic: 0.75 us -> none  [frequency_shards(): image = raw / jnp.sqrt(mean_square + 1e-06)[:, None, None]]
  transfers between devices with their start and end apart: 21 -> 21, of which waited for: 11 -> 10; matrix products, arithmetic and copies ran while one was open for 5% -> 6% of each run, Pallas kernels for 30% -> 28%
where the time goes in v3:
time: 72.2 us; the launch traced here: 71.9 us
  starting transfers between devices  25.2 us (35%)
  Pallas kernels  21.5 us (30%)
  waiting for transfers between devices  18.4 us (25%)
  local copies, waits for them, and re-layouts  3.07 us (4%)
  between operations  2.81 us (4%)
  other arithmetic  0.91 us (1%)
    ppermute x21, starting transfers between devices, send(): return lax.ppermute(value, 'strip', pairs)  25.2 us
    pallas_call x7, Pallas kernels, call(): pl.pallas_call(kernel, out_shape=outs, in_specs=[smem] + [vmem] * (len(op...  21.5 us
    ppermute x21, waiting for transfers between devices, send(): return lax.ppermute(value, 'strip', pairs)  18.4 us
  transfers between devices with their start and end apart: 21, of which 10 were waited for; matrix products, arithmetic and copies ran while one was open for 6% of the time, Pallas kernels for 28%

profile of v3, /device:TPU:0, one launch (start us, length us, event | category | flops | bytes accessed | tf_op | source)
XLA Modules:
  0.0 71.9 jit_solution(8234675717480412121)
XLA Ops:
  0.6 5.1 %collective-permute-start.2 = (s32[2,16,1024]{2,1,0:T(8,128)}, s32[2,16,1024]{2,1,0:T(8,128)S(1)}, u32[]{:S(2)}, u32[]{:S(2)}) collective-permute-start(s32[2,16,1024]{2,1,0:T(8,128)} %param.7), channel_id=1, source_target_pairs={{0,12},{1,13},{2,6},{3,7},{4,0},{5,1},{6,10},{7,11},{8,4},{9,5},{1... | collective-permute-start | bytes 393224 | tf_op jit(solution)/shard_map/ppermute | solution.py:459
  5.7 1.2 %dynamic-slice_bitcast_fusion = (f32[2,16,1024]{2,1,0:T(8,128)S(1)}, f32[2,16,1024]{2,1,0:T(8,128)S(1)}, f32[2,16,1024]{2,1,0:T(8,128)S(1)}, f32[2,16,1024]{2,1,0:T(8,128)S(1)}) fusion(f32[4,2,16,1024]{3,2,1,0:T(8,128)} %param.6, s32[]{:T(128)S(6)} %select_n.78, s32[]{:T(128)S(6)} %select_n.74, s32[]{:T(128)S(6)} %select_n.73, s32[]{:T(128)S(6)} %select_n.77), kind=kLoop, calls=%fused_computation.1 | loop fusion | bytes 1048592 | tf_op jit(solution)/shard_map/jit(dynamic_index_in_dim)/squeeze | solution.py:471
  6.9 0.7 collective-permute-start
  7.7 1.1 %collective-permute-done.2 = s32[2,16,1024]{2,1,0:T(8,128)S(1)} collective-permute-done((s32[2,16,1024]{2,1,0:T(8,128)}, s32[2,16,1024]{2,1,0:T(8,128)S(1)}, u32[]{:S(2)}, u32[]{:S(2)}) %collective-permute-start.2) | collective-permute-done | bytes 131104 | tf_op jit(solution)/shard_map/ppermute | solution.py:459
  8.8 2.2 %collective-permute-start.5 = (s32[2,16,1024]{2,1,0:T(8,128)S(1)}, s32[2,16,1024]{2,1,0:T(8,128)S(1)}, u32[]{:S(2)}, u32[]{:S(2)}) collective-permute-start(s32[2,16,1024]{2,1,0:T(8,128)S(1)} %get-tuple-element.39.own), channel_id=1, source_target_pairs={{0,2},{1,3},{2,0},{3,1},{4,6},{5,7},{6,4},{7,5},{8,10},{9,11},{10,... | collective-permute-start | bytes 393224 | tf_op jit(solution)/shard_map/ppermute | solution.py:459
  11.1 1.3 %dynamic_slice.27 = s32[1,1]{1,0:T(1,128)} dynamic-slice(s32[4,4]{1,0:T(4,128)} %param.8, s32[]{:T(128)S(6)} %select_n.81, s32[]{:T(128)S(6)} %select_n.73), dynamic_slice_sizes={1,1} | dynamic-slice | bytes 12 | tf_op jit(solution)/shard_map/dynamic_slice | solution.py:503
  13.8 1.3 %collective-permute-start.4 = (f32[2,16,1024]{2,1,0:T(8,128)S(1)}, f32[2,16,1024]{2,1,0:T(8,128)S(1)}, u32[]{:S(2)}, u32[]{:S(2)}) collective-permute-start(f32[2,16,1024]{2,1,0:T(8,128)S(1)} %get-tuple-element.38), channel_id=1, source_target_pairs={{0,3},{1,2},{2,5},{3,4},{4,7},{5,6},{6,9},{7,8},{8,11},{9,10},{10,... | collective-permute-start | bytes 393224 | tf_op jit(solution)/shard_map/ppermute | solution.py:459
  15.8 0.6 dynamic_slice.29
  16.5 0.8 %collective-permute-start.6 = (s32[2,2,16,1024]{3,2,1,0:T(8,128)S(1)}, s32[2,2,16,1024]{3,2,1,0:T(8,128)S(1)}, u32[]{:S(2)}, u32[]{:S(2)}) collective-permute-start(s32[2,2,16,1024]{3,2,1,0:T(8,128)S(1)} %pad_add_fusion), channel_id=1, source_target_pairs={{0,1},{1,0},{2,3},{3,2},{4,5},{5,4},{6,7},{7,6},{8,9},{9,8},{10,11... | collective-permute-start | bytes 786440 | tf_op jit(solution)/shard_map/ppermute | solution.py:459
  17.3 0.7 multiply_cosine_fusion
  18.5 1.0 %shard_map.77.cells = s32[2,8,64,128]{3,2,1,0:T(8,128)S(1)} custom-call(s32[2]{0:T(128)S(1)} %pad_add_fusion.1.lane_ref, s32[2,16,1024]{2,1,0:T(8,128)S(1)} %get-tuple-element.39.own, s32[2,16,1024]{2,1,0:T(8,128)S(1)} %collective-permute-done.5.two, s32[2,2,16,1024]{3,2,1,0:T(8,128)S(1)} %collective-permute-done.6.pair), custom_call_target="tpu_custom_call" | custom-call | flops 524288 | bytes 2097152 | tf_op jit(solution)/shard_map/pallas_call | solution.py:428
  20.0 1.7 %collective-permute-start.9 = (s32[2,16,1024]{2,1,0:T(8,128)S(1)}, s32[2,16,1024]{2,1,0:T(8,128)S(1)}, u32[]{:S(2)}, u32[]{:S(2)}) collective-permute-start(s32[2,16,1024]{2,1,0:T(8,128)S(1)} %get-tuple-element.48.own), channel_id=1, source_target_pairs={{0,3},{1,2},{2,1},{3,0},{4,7},{5,6},{6,5},{7,4},{8,11},{9,10},{10,... | collective-permute-start | bytes 393224 | tf_op jit(solution)/shard_map/ppermute | solution.py:459
  21.8 1.0 %collective-permute-done.3.w2 = f32[2,16,1024]{2,1,0:T(8,128)S(1)} collective-permute-done((f32[2,16,1024]{2,1,0:T(8,128)S(1)}, f32[2,16,1024]{2,1,0:T(8,128)S(1)}, u32[]{:S(2)}, u32[]{:S(2)}) %collective-permute-start.3) | collective-permute-done | bytes 131104 | tf_op jit(solution)/shard_map/ppermute | solution.py:459
  22.8 1.9 %collective-permute-done.4.w3 = f32[2,16,1024]{2,1,0:T(8,128)S(1)} collective-permute-done((f32[2,16,1024]{2,1,0:T(8,128)S(1)}, f32[2,16,1024]{2,1,0:T(8,128)S(1)}, u32[]{:S(2)}, u32[]{:S(2)}) %collective-permute-start.4) | collective-permute-done | bytes 131104 | tf_op jit(solution)/shard_map/ppermute | solution.py:459
  24.7 8.4 %shard_map.78 = (f32[2,8,64,128]{3,2,1,0:T(8,128)S(1)}, f32[3,16,1024]{2,1,0:T(8,128)S(1)}, f32[3,16,1024]{2,1,0:T(8,128)S(1)}, f32[3,16,1024]{2,1,0:T(8,128)S(1)}, f32[3,16,1024]{2,1,0:T(8,128)S(1)}) custom-call(s32[2]{0:T(128)S(1)} %pad_add_fusion.1.lane_ref, f32[2,16,1024]{2,1,0:T(8,128)S(1)} %collective-permute-done.w0, ...), custom_call_target="tpu_custom_call" | custom-call | flops 10485760 | bytes 41943040 | tf_op jit(solution)/shard_map/pallas_call | solution.py:428
  33.2 0.7 collective-permute-start.10
  34.2 3.0 %collective-permute-start.12 = (f32[3,16,1024]{2,1,0:T(8,128)S(1)}, f32[3,16,1024]{2,1,0:T(8,128)S(1)}, u32[]{:S(2)}, u32[]{:S(2)}) collective-permute-start(f32[3,16,1024]{2,1,0:T(8,128)S(1)} %get-tuple-element.58), channel_id=1, source_target_pairs={{0,14},{1,15},{2,0},{3,1},{4,2},{5,3},{6,4},{7,5},{8,6},{9,7},{10,... | collective-permute-start | bytes 589832 | tf_op jit(solution)/shard_map/ppermute | solution.py:459
  37.2 1.0 %shard_map.79.cells = s32[2,8,64,128]{3,2,1,0:T(8,128)S(1)} custom-call(s32[2]{0:T(128)S(1)} %pad_add_fusion.1.lane_ref, s32[2,16,1024]{2,1,0:T(8,128)S(1)} %get-tuple-element.48.own, s32[2,16,1024]{2,1,0:T(8,128)S(1)} %collective-permute-done.7.two, s32[2,16,1024]{2,1,0:T(8,128)S(1)} %collective-permute-done.8.one, ...), custom_call_target="tpu_custom_call" | custom-call | flops 524288 | bytes 2097152 | tf_op jit(solution)/shard_map/pallas_call | solution.py:428
  38.2 7.9 %shard_map.80 = (f32[3,16,1024]{2,1,0:T(8,128)S(1)}, f32[3,16,1024]{2,1,0:T(8,128)S(1)}, f32[3,16,1024]{2,1,0:T(8,128)S(1)}, f32[3,16,1024]{2,1,0:T(8,128)S(1)}) custom-call(s32[2]{0:T(128)S(1)} %pad_add_fusion.1.lane_ref, f32[2,8,64,128]{3,2,1,0:T(8,128)S(1)} %get-tuple-element.42.wave, s32[2,8,64,128]{3,2,1,0:T(8,128)S(1)} %shard_map.79.cells, ...), custom_call_target="tpu_custom_call" | custom-call | flops 10485760 | bytes 41943040 | tf_op jit(solution)/shard_map/pallas_call | solution.py:428
  46.1 0.9 %collective-permute-done.13.n3 = f32[3,16,1024]{2,1,0:T(8,128)S(1)} collective-permute-done((f32[3,16,1024]{2,1,0:T(8,128)S(1)}, f32[3,16,1024]{2,1,0:T(8,128)S(1)}, u32[]{:S(2)}, u32[]{:S(2)}) %collective-permute-start.13) | collective-permute-done | bytes 196640 | tf_op jit(solution)/shard_map/ppermute | solution.py:459
  47.1 2.7 %collective-permute-start.14 = (f32[3,16,1024]{2,1,0:T(8,128)S(1)}, f32[3,16,1024]{2,1,0:T(8,128)S(1)}, u32[]{:S(2)}, u32[]{:S(2)}) collective-permute-start(f32[3,16,1024]{2,1,0:T(8,128)S(1)} %get-tuple-element.60), channel_id=1, source_target_pairs={{0,4},{1,5},{2,2},{3,3},{4,8},{5,9},{6,6},{7,7},{8,12},{9,13},{10,... | collective-permute-start | bytes 589832 | tf_op jit(solution)/shard_map/ppermute | solution.py:459
  49.8 0.5 collective-permute-start.16
  50.4 0.5 collective-permute-start.17
  50.9 7.7 %collective-permute-done.14.m0 = f32[3,16,1024]{2,1,0:T(8,128)S(1)} collective-permute-done((f32[3,16,1024]{2,1,0:T(8,128)S(1)}, f32[3,16,1024]{2,1,0:T(8,128)S(1)}, u32[]{:S(2)}, u32[]{:S(2)}) %collective-permute-start.14) | collective-permute-done | bytes 196640 | tf_op jit(solution)/shard_map/ppermute | solution.py:459
  58.5 2.5 %collective-permute-done.15.m1 = f32[3,16,1024]{2,1,0:T(8,128)S(1)} collective-permute-done((f32[3,16,1024]{2,1,0:T(8,128)S(1)}, f32[3,16,1024]{2,1,0:T(8,128)S(1)}, u32[]{:S(2)}, u32[]{:S(2)}) %collective-permute-start.15) | collective-permute-done | bytes 196640 | tf_op jit(solution)/shard_map/ppermute | solution.py:459
  61.0 2.0 %collective-permute-done.17.m3 = f32[3,16,1024]{2,1,0:T(8,128)S(1)} collective-permute-done((f32[3,16,1024]{2,1,0:T(8,128)S(1)}, f32[3,16,1024]{2,1,0:T(8,128)S(1)}, u32[]{:S(2)}, u32[]{:S(2)}) %collective-permute-start.17) | collective-permute-done | bytes 196640 | tf_op jit(solution)/shard_map/ppermute | solution.py:459
  63.0 0.7 %shard_map.81 = (f32[2,16,1024]{2,1,0:T(8,128)S(1)}, f32[8,128]{1,0:T(8,128)S(1)}) custom-call(s32[2]{0:T(128)S(1)} %pad_add_fusion.1.lane_ref, f32[3,16,1024]{2,1,0:T(8,128)S(1)} %collective-permute-done.14.m0, f32[3,16,1024]{2,1,0:T(8,128)S(1)} %collective-permute-done.15.m1, f32[3,16,1024]{2,1,0:T(8,128)S(1)} %collective-permute-done.16.m2, ...), custom_call_target="tpu_custom_call" | custom-call | flops 262144 | bytes 1048576 | tf_op jit(solution)/shard_map/pallas_call | solution.py:428
  63.8 0.6 collective-permute-start.18
  64.4 1.0 %collective-permute-start.19 = (f32[8,128]{1,0:T(8,128)S(1)}, f32[8,128]{1,0:T(8,128)S(1)}, u32[]{:S(2)}, u32[]{:S(2)}) collective-permute-start(f32[8,128]{1,0:T(8,128)S(1)} %get-tuple-element.70.s0), channel_id=1, source_target_pairs={{2,4},{3,5},{4,2},{5,3},{6,8},{7,9},{8,6},{9,7},{10,12},{11,13},{1... | collective-permute-start | bytes 12296 | tf_op jit(solution)/shard_map/ppermute | solution.py:459
  65.4 3.1 %collective-permute-start.20 = (f32[8,128]{1,0:T(8,128)S(1)}, f32[8,128]{1,0:T(8,128)S(1)}, u32[]{:S(2)}, u32[]{:S(2)}) collective-permute-start(f32[8,128]{1,0:T(8,128)S(1)} %get-tuple-element.70.s0), channel_id=1, source_target_pairs={{2,5},{3,4},{4,3},{5,2},{6,9},{7,8},{8,7},{9,6},{10,13},{11,12},{1... | collective-permute-start | bytes 12296 | tf_op jit(solution)/shard_map/ppermute | solution.py:459
  68.5 1.8 %shard_map.82 = (f32[4,2,16,1024]{3,2,1,0:T(8,128)}, f32[2,16,1024]{2,1,0:T(8,128)S(1)}) custom-call(s32[2]{0:T(128)S(1)} %pad_add_fusion.1.lane_ref, f32[3,16,1024]{2,1,0:T(8,128)S(1)} %collective-permute-done.14.m0, f32[3,16,1024]{2,1,0:T(8,128)S(1)} %collective-permute-done.15.m1, f32[3,16,1024]{2,1,0:T(8,128)S(1)} %collective-permute-done.16.m2, ...), custom_call_target="tpu_custom_call" | custom-call | flops 1048576 | bytes 4194304 | tf_op jit(solution)/shard_map/pallas_call | solution.py:428
  71.1 0.8 %shard_map.83 = f32[2,16,1024]{2,1,0:T(8,128)} custom-call(s32[1]{0:T(128)} %constant.67.clone.1.cells_ref, f32[2,16,1024]{2,1,0:T(8,128)S(1)} %get-tuple-element.69.raw, f32[8,128]{1,0:T(8,128)S(1)} %get-tuple-element.70.s0, f32[8,128]{1,0:T(8,128)S(1)} %collective-permute-done.18.s1, f32[8,128]{1,0:T(8,128)S(1)} %collective-permute-done.19.s2, ...), custom_call_target="tpu_custom_call" | custom-call | flops 131072 | bytes 524288 | tf_op jit(solution)/shard_map/pallas_call | solution.py:428
  (38 shorter events, 2.7 us)
Async XLA Ops:
  0.6 17.4 %copy-start = (f32[16,16,2,13]{1,2,3,0:T(2,128)S(1)}, f32[16,16,2,13]{1,2,3,0:T(2,128)}, u32[]{:S(2)}) copy-start(f32[16,16,2,13]{1,2,3,0:T(2,128)} %param.9) | copy-start | bytes 79876
  0.6 8.2 %collective-permute-start.2 = (s32[2,16,1024]{2,1,0:T(8,128)}, s32[2,16,1024]{2,1,0:T(8,128)S(1)}, u32[]{:S(2)}, u32[]{:S(2)}) collective-permute-start(s32[2,16,1024]{2,1,0:T(8,128)} %param.7), channel_id=1, source_target_pairs={{0,12},{1,13},{2,6},{3,7},{4,0},{5,1},{6,10},{7,11},{8,4},{9,5},{1... | collective-permute-start | bytes 393224 | tf_op jit(solution)/shard_map/ppermute | solution.py:459
  5.7 3.1 %copy-start.1 = (s32[2,16,1024]{2,1,0:T(8,128)S(1)}, s32[2,16,1024]{2,1,0:T(8,128)}, u32[]{:S(2)}) copy-start(s32[2,16,1024]{2,1,0:T(8,128)} %param.7) | copy-start | bytes 393220
  6.9 12.9 %collective-permute-start = (f32[2,16,1024]{2,1,0:T(8,128)S(1)}, f32[2,16,1024]{2,1,0:T(8,128)S(1)}, u32[]{:S(2)}, u32[]{:S(2)}) collective-permute-start(f32[2,16,1024]{2,1,0:T(8,128)S(1)} %get-tuple-element.74), channel_id=1, source_target_pairs={{0,0},{1,1},{2,6},{3,7},{4,4},{5,5},{6,10},{7,11},{8,8},{9,9},{10,... | collective-permute-start | bytes 393224 | tf_op jit(solution)/shard_map/ppermute | solution.py:459
  7.6 12.4 %collective-permute-start.1 = (f32[2,16,1024]{2,1,0:T(8,128)S(1)}, f32[2,16,1024]{2,1,0:T(8,128)S(1)}, u32[]{:S(2)}, u32[]{:S(2)}) collective-permute-start(f32[2,16,1024]{2,1,0:T(8,128)S(1)} %get-tuple-element.73), channel_id=1, source_target_pairs={{0,1},{1,0},{2,7},{3,6},{4,5},{5,4},{6,11},{7,10},{8,9},{9,8},{10,... | collective-permute-start | bytes 393224 | tf_op jit(solution)/shard_map/ppermute | solution.py:459
  8.8 7.6 %collective-permute-start.5 = (s32[2,16,1024]{2,1,0:T(8,128)S(1)}, s32[2,16,1024]{2,1,0:T(8,128)S(1)}, u32[]{:S(2)}, u32[]{:S(2)}) collective-permute-start(s32[2,16,1024]{2,1,0:T(8,128)S(1)} %get-tuple-element.39.own), channel_id=1, source_target_pairs={{0,2},{1,3},{2,0},{3,1},{4,6},{5,7},{6,4},{7,5},{8,10},{9,11},{10,... | collective-permute-start | bytes 393224 | tf_op jit(solution)/shard_map/ppermute | solution.py:459
  13.7 2.1 %copy-start.3 = (f32[16]{0:T(128)S(1)}, f32[16]{0:T(128)}, u32[]{:S(2)}) copy-start(f32[16]{0:T(128)} %param.10) | copy-start | bytes 196
  13.7 9.1 %collective-permute-start.3 = (f32[2,16,1024]{2,1,0:T(8,128)S(1)}, f32[2,16,1024]{2,1,0:T(8,128)S(1)}, u32[]{:S(2)}, u32[]{:S(2)}) collective-permute-start(f32[2,16,1024]{2,1,0:T(8,128)S(1)} %get-tuple-element.37), channel_id=1, source_target_pairs={{0,2},{1,3},{2,4},{3,5},{4,6},{5,7},{6,8},{7,9},{8,10},{9,11},{10,... | collective-permute-start | bytes 393224 | tf_op jit(solution)/shard_map/ppermute | solution.py:459
  13.8 10.9 %collective-permute-start.4 = (f32[2,16,1024]{2,1,0:T(8,128)S(1)}, f32[2,16,1024]{2,1,0:T(8,128)S(1)}, u32[]{:S(2)}, u32[]{:S(2)}) collective-permute-start(f32[2,16,1024]{2,1,0:T(8,128)S(1)} %get-tuple-element.38), channel_id=1, source_target_pairs={{0,3},{1,2},{2,5},{3,4},{4,7},{5,6},{6,9},{7,8},{8,11},{9,10},{10,... | collective-permute-start | bytes 393224 | tf_op jit(solution)/shard_map/ppermute | solution.py:459
  16.5 0.9 %copy-start.2 = (f32[16]{0:T(128)S(1)}, f32[16]{0:T(128)}, u32[]{:S(2)}) copy-start(f32[16]{0:T(128)} %param.11) | copy-start | bytes 196
  16.5 2.0 %collective-permute-start.6 = (s32[2,2,16,1024]{3,2,1,0:T(8,128)S(1)}, s32[2,2,16,1024]{3,2,1,0:T(8,128)S(1)}, u32[]{:S(2)}, u32[]{:S(2)}) collective-permute-start(s32[2,2,16,1024]{3,2,1,0:T(8,128)S(1)} %pad_add_fusion), channel_id=1, source_target_pairs={{0,1},{1,0},{2,3},{3,2},{4,5},{5,4},{6,7},{7,6},{8,9},{9,8},{10,11... | collective-permute-start | bytes 786440 | tf_op jit(solution)/shard_map/ppermute | solution.py:459
  19.5 13.7 %collective-permute-start.7 = (s32[2,16,1024]{2,1,0:T(8,128)S(1)}, s32[2,16,1024]{2,1,0:T(8,128)S(1)}, u32[]{:S(2)}, u32[]{:S(2)}) collective-permute-start(s32[2,16,1024]{2,1,0:T(8,128)S(1)} %get-tuple-element.48.own), channel_id=1, source_target_pairs={{0,2},{1,3},{2,0},{3,1},{4,6},{5,7},{6,4},{7,5},{8,10},{9,11},{10,... | collective-permute-start | bytes 393224 | tf_op jit(solution)/shard_map/ppermute | solution.py:459
  19.8 13.3 %collective-permute-start.8 = (s32[2,16,1024]{2,1,0:T(8,128)S(1)}, s32[2,16,1024]{2,1,0:T(8,128)S(1)}, u32[]{:S(2)}, u32[]{:S(2)}) collective-permute-start(s32[2,16,1024]{2,1,0:T(8,128)S(1)} %get-tuple-element.48.own), channel_id=1, source_target_pairs={{0,1},{1,0},{2,3},{3,2},{4,5},{5,4},{6,7},{7,6},{8,9},{9,8},{10,11... | collective-permute-start | bytes 393224 | tf_op jit(solution)/shard_map/ppermute | solution.py:459
  20.0 13.2 %collective-permute-start.9 = (s32[2,16,1024]{2,1,0:T(8,128)S(1)}, s32[2,16,1024]{2,1,0:T(8,128)S(1)}, u32[]{:S(2)}, u32[]{:S(2)}) collective-permute-start(s32[2,16,1024]{2,1,0:T(8,128)S(1)} %get-tuple-element.48.own), channel_id=1, source_target_pairs={{0,3},{1,2},{2,1},{3,0},{4,7},{5,6},{6,5},{7,4},{8,11},{9,10},{10,... | collective-permute-start | bytes 393224 | tf_op jit(solution)/shard_map/ppermute | solution.py:459
  33.2 12.9 %collective-permute-start.10 = (f32[3,16,1024]{2,1,0:T(8,128)S(1)}, f32[3,16,1024]{2,1,0:T(8,128)S(1)}, u32[]{:S(2)}, u32[]{:S(2)}) collective-permute-start(f32[3,16,1024]{2,1,0:T(8,128)S(1)} %get-tuple-element.56), channel_id=1, source_target_pairs={{0,0},{1,1},{2,14},{3,15},{4,4},{5,5},{6,2},{7,3},{8,8},{9,9},{10,... | collective-permute-start | bytes 589832 | tf_op jit(solution)/shard_map/ppermute | solution.py:459
  33.9 12.3 %collective-permute-start.11 = (f32[3,16,1024]{2,1,0:T(8,128)S(1)}, f32[3,16,1024]{2,1,0:T(8,128)S(1)}, u32[]{:S(2)}, u32[]{:S(2)}) collective-permute-start(f32[3,16,1024]{2,1,0:T(8,128)S(1)} %get-tuple-element.57), channel_id=1, source_target_pairs={{0,1},{1,0},{2,15},{3,14},{4,5},{5,4},{6,3},{7,2},{8,9},{9,8},{10,... | collective-permute-start | bytes 589832 | tf_op jit(solution)/shard_map/ppermute | solution.py:459
  34.2 11.9 %collective-permute-start.12 = (f32[3,16,1024]{2,1,0:T(8,128)S(1)}, f32[3,16,1024]{2,1,0:T(8,128)S(1)}, u32[]{:S(2)}, u32[]{:S(2)}) collective-permute-start(f32[3,16,1024]{2,1,0:T(8,128)S(1)} %get-tuple-element.58), channel_id=1, source_target_pairs={{0,14},{1,15},{2,0},{3,1},{4,2},{5,3},{6,4},{7,5},{8,6},{9,7},{10,... | collective-permute-start | bytes 589832 | tf_op jit(solution)/shard_map/ppermute | solution.py:459
  37.2 9.9 %collective-permute-start.13 = (f32[3,16,1024]{2,1,0:T(8,128)S(1)}, f32[3,16,1024]{2,1,0:T(8,128)S(1)}, u32[]{:S(2)}, u32[]{:S(2)}) collective-permute-start(f32[3,16,1024]{2,1,0:T(8,128)S(1)} %get-tuple-element.59), channel_id=1, source_target_pairs={{0,15},{1,14},{2,1},{3,0},{4,3},{5,2},{6,5},{7,4},{8,7},{9,6},{10,... | collective-permute-start | bytes 589832 | tf_op jit(solution)/shard_map/ppermute | solution.py:459
  47.1 11.4 %collective-permute-start.14 = (f32[3,16,1024]{2,1,0:T(8,128)S(1)}, f32[3,16,1024]{2,1,0:T(8,128)S(1)}, u32[]{:S(2)}, u32[]{:S(2)}) collective-permute-start(f32[3,16,1024]{2,1,0:T(8,128)S(1)} %get-tuple-element.60), channel_id=1, source_target_pairs={{0,4},{1,5},{2,2},{3,3},{4,8},{5,9},{6,6},{7,7},{8,12},{9,13},{10,... | collective-permute-start | bytes 589832 | tf_op jit(solution)/shard_map/ppermute | solution.py:459
  49.8 11.2 %collective-permute-start.15 = (f32[3,16,1024]{2,1,0:T(8,128)S(1)}, f32[3,16,1024]{2,1,0:T(8,128)S(1)}, u32[]{:S(2)}, u32[]{:S(2)}) collective-permute-start(f32[3,16,1024]{2,1,0:T(8,128)S(1)} %get-tuple-element.61), channel_id=1, source_target_pairs={{0,5},{1,4},{2,3},{3,2},{4,9},{5,8},{6,7},{7,6},{8,13},{9,12},{10,... | collective-permute-start | bytes 589832 | tf_op jit(solution)/shard_map/ppermute | solution.py:459
  49.8 11.2 %collective-permute-start.16 = (f32[3,16,1024]{2,1,0:T(8,128)S(1)}, f32[3,16,1024]{2,1,0:T(8,128)S(1)}, u32[]{:S(2)}, u32[]{:S(2)}) collective-permute-start(f32[3,16,1024]{2,1,0:T(8,128)S(1)} %get-tuple-element.62), channel_id=1, source_target_pairs={{0,2},{1,3},{2,4},{3,5},{4,6},{5,7},{6,8},{7,9},{8,10},{9,11},{10,... | collective-permute-start | bytes 589832 | tf_op jit(solution)/shard_map/ppermute | solution.py:459
  50.4 12.6 %collective-permute-start.17 = (f32[3,16,1024]{2,1,0:T(8,128)S(1)}, f32[3,16,1024]{2,1,0:T(8,128)S(1)}, u32[]{:S(2)}, u32[]{:S(2)}) collective-permute-start(f32[3,16,1024]{2,1,0:T(8,128)S(1)} %get-tuple-element.63), channel_id=1, source_target_pairs={{0,3},{1,2},{2,5},{3,4},{4,7},{5,6},{6,9},{7,8},{8,11},{9,10},{10,... | collective-permute-start | bytes 589832 | tf_op jit(solution)/shard_map/ppermute | solution.py:459
  63.8 6.6 %collective-permute-start.18 = (f32[8,128]{1,0:T(8,128)S(1)}, f32[8,128]{1,0:T(8,128)S(1)}, u32[]{:S(2)}, u32[]{:S(2)}) collective-permute-start(f32[8,128]{1,0:T(8,128)S(1)} %get-tuple-element.70.s0), channel_id=1, source_target_pairs={{2,3},{3,2},{4,5},{5,4},{6,7},{7,6},{8,9},{9,8},{10,11},{11,10},{1... | collective-permute-start | bytes 12296 | tf_op jit(solution)/shard_map/ppermute | solution.py:459
  64.4 6.3 %collective-permute-start.19 = (f32[8,128]{1,0:T(8,128)S(1)}, f32[8,128]{1,0:T(8,128)S(1)}, u32[]{:S(2)}, u32[]{:S(2)}) collective-permute-start(f32[8,128]{1,0:T(8,128)S(1)} %get-tuple-element.70.s0), channel_id=1, source_target_pairs={{2,4},{3,5},{4,2},{5,3},{6,8},{7,9},{8,6},{9,7},{10,12},{11,13},{1... | collective-permute-start | bytes 12296 | tf_op jit(solution)/shard_map/ppermute | solution.py:459
  65.4 5.7 %collective-permute-start.20 = (f32[8,128]{1,0:T(8,128)S(1)}, f32[8,128]{1,0:T(8,128)S(1)}, u32[]{:S(2)}, u32[]{:S(2)}) collective-permute-start(f32[8,128]{1,0:T(8,128)S(1)} %get-tuple-element.70.s0), channel_id=1, source_target_pairs={{2,5},{3,4},{4,3},{5,2},{6,9},{7,8},{8,7},{9,6},{10,13},{11,12},{1... | collective-permute-start | bytes 12296 | tf_op jit(solution)/shard_map/ppermute | solution.py:459

commit v4 on v3

--- a/solution.py
+++ b/solution.py
@@ -207,25 +207,21 @@
 
 
 def advance(src, other, tiles, first=False):
-    edges = [rim(src, plane, tiles) for plane in range(2)]
-    above = [e[1] for e in edges]
-    present = [e[2] for e in edges]
-    for i in range(SUB):
-        for plane in range(2):
+    for plane in range(2):
+        seam, above, present = rim(src, plane, tiles)
+        for i in range(SUB):
             if i < SUB - 1:
                 below = [src[(plane,) + cell(i + 1, j)] for j in range(tiles)]
-                pairs = [present[plane][j] + below[j] for j in range(tiles)]
+                pairs = [present[j] + below[j] for j in range(tiles)]
             else:
-                below = None
-                pairs = edges[plane][0]
-            h = across([pairs[j] + above[plane][j] for j in range(tiles)])
-            above[plane] = pairs
+                below, pairs = None, seam
+            h = across([pairs[j] + above[j] for j in range(tiles)])
+            above = pairs
             for j in range(tiles):
                 at = (plane,) + cell(i, j)
-                v = present[plane][j]
-                u = v - 0.125 * h[j] if first else (v + v) - (0.25 * h[j] + other[at])
-                other[at] = u
-            present[plane] = below
+                v = present[j]
+                other[at] = v - 0.125 * h[j] if first else (v + v) - (0.25 * h[j] + other[at])
+            present = below
 
 
 def add_orders(lower, upper, total, cells, table, k, tiles, first=False):

time: 72.2 us -> 72.2 us (level)
  no operation moved by 1% of the time
where the time goes in v4:
time: 72.2 us; the launch traced here: 71.9 us
  starting transfers between devices  25.2 us (35%)
  Pallas kernels  21.6 us (30%)
  waiting for transfers between devices  18.4 us (25%)
  local copies, waits for them, and re-layouts  3.07 us (4%)
  between operations  2.81 us (4%)
  other arithmetic  0.91 us (1%)
    ppermute x21, starting transfers between devices, send(): return lax.ppermute(value, 'strip', pairs)  25.2 us
    pallas_call x7, Pallas kernels, call(): pl.pallas_call(kernel, out_shape=outs, in_specs=[smem] + [vmem] * (len(op...  21.6 us
    ppermute x21, waiting for transfers between devices, send(): return lax.ppermute(value, 'strip', pairs)  18.4 us
  transfers between devices with their start and end apart: 21, of which 10 were waited for; matrix products, arithmetic and copies ran while one was open for 6% of the time, Pallas kernels for 28%

profile of v4, /device:TPU:0, one launch (start us, length us, event | category | flops | bytes accessed | tf_op | source)
XLA Modules:
  0.0 71.9 jit_solution(16113448848015766333)
XLA Ops:
  0.6 5.1 %collective-permute-start.2 = (s32[2,16,1024]{2,1,0:T(8,128)}, s32[2,16,1024]{2,1,0:T(8,128)S(1)}, u32[]{:S(2)}, u32[]{:S(2)}) collective-permute-start(s32[2,16,1024]{2,1,0:T(8,128)} %param.7), channel_id=1, source_target_pairs={{0,12},{1,13},{2,6},{3,7},{4,0},{5,1},{6,10},{7,11},{8,4},{9,5},{1... | collective-permute-start | bytes 393224 | tf_op jit(solution)/shard_map/ppermute | solution.py:455
  5.7 1.2 %dynamic-slice_bitcast_fusion = (f32[2,16,1024]{2,1,0:T(8,128)S(1)}, f32[2,16,1024]{2,1,0:T(8,128)S(1)}, f32[2,16,1024]{2,1,0:T(8,128)S(1)}, f32[2,16,1024]{2,1,0:T(8,128)S(1)}) fusion(f32[4,2,16,1024]{3,2,1,0:T(8,128)} %param.6, s32[]{:T(128)S(6)} %select_n.78, s32[]{:T(128)S(6)} %select_n.74, s32[]{:T(128)S(6)} %select_n.73, s32[]{:T(128)S(6)} %select_n.77), kind=kLoop, calls=%fused_computation.1 | loop fusion | bytes 1048592 | tf_op jit(solution)/shard_map/jit(dynamic_index_in_dim)/squeeze | solution.py:467
  6.9 0.7 collective-permute-start
  7.7 1.1 %collective-permute-done.2 = s32[2,16,1024]{2,1,0:T(8,128)S(1)} collective-permute-done((s32[2,16,1024]{2,1,0:T(8,128)}, s32[2,16,1024]{2,1,0:T(8,128)S(1)}, u32[]{:S(2)}, u32[]{:S(2)}) %collective-permute-start.2) | collective-permute-done | bytes 131104 | tf_op jit(solution)/shard_map/ppermute | solution.py:455
  8.8 2.2 %collective-permute-start.5 = (s32[2,16,1024]{2,1,0:T(8,128)S(1)}, s32[2,16,1024]{2,1,0:T(8,128)S(1)}, u32[]{:S(2)}, u32[]{:S(2)}) collective-permute-start(s32[2,16,1024]{2,1,0:T(8,128)S(1)} %get-tuple-element.39.own), channel_id=1, source_target_pairs={{0,2},{1,3},{2,0},{3,1},{4,6},{5,7},{6,4},{7,5},{8,10},{9,11},{10,... | collective-permute-start | bytes 393224 | tf_op jit(solution)/shard_map/ppermute | solution.py:455
  11.1 1.3 %dynamic_slice.27 = s32[1,1]{1,0:T(1,128)} dynamic-slice(s32[4,4]{1,0:T(4,128)} %param.8, s32[]{:T(128)S(6)} %select_n.81, s32[]{:T(128)S(6)} %select_n.73), dynamic_slice_sizes={1,1} | dynamic-slice | bytes 12 | tf_op jit(solution)/shard_map/dynamic_slice | solution.py:499
  13.8 1.3 %collective-permute-start.4 = (f32[2,16,1024]{2,1,0:T(8,128)S(1)}, f32[2,16,1024]{2,1,0:T(8,128)S(1)}, u32[]{:S(2)}, u32[]{:S(2)}) collective-permute-start(f32[2,16,1024]{2,1,0:T(8,128)S(1)} %get-tuple-element.38), channel_id=1, source_target_pairs={{0,3},{1,2},{2,5},{3,4},{4,7},{5,6},{6,9},{7,8},{8,11},{9,10},{10,... | collective-permute-start | bytes 393224 | tf_op jit(solution)/shard_map/ppermute | solution.py:455
  15.8 0.6 dynamic_slice.29
  16.5 0.8 %collective-permute-start.6 = (s32[2,2,16,1024]{3,2,1,0:T(8,128)S(1)}, s32[2,2,16,1024]{3,2,1,0:T(8,128)S(1)}, u32[]{:S(2)}, u32[]{:S(2)}) collective-permute-start(s32[2,2,16,1024]{3,2,1,0:T(8,128)S(1)} %pad_add_fusion), channel_id=1, source_target_pairs={{0,1},{1,0},{2,3},{3,2},{4,5},{5,4},{6,7},{7,6},{8,9},{9,8},{10,11... | collective-permute-start | bytes 786440 | tf_op jit(solution)/shard_map/ppermute | solution.py:455
  17.3 0.7 multiply_cosine_fusion
  18.5 1.0 %shard_map.77.cells = s32[2,8,64,128]{3,2,1,0:T(8,128)S(1)} custom-call(s32[2]{0:T(128)S(1)} %pad_add_fusion.1.lane_ref, s32[2,16,1024]{2,1,0:T(8,128)S(1)} %get-tuple-element.39.own, s32[2,16,1024]{2,1,0:T(8,128)S(1)} %collective-permute-done.5.two, s32[2,2,16,1024]{3,2,1,0:T(8,128)S(1)} %collective-permute-done.6.pair), custom_call_target="tpu_custom_call" | custom-call | flops 524288 | bytes 2097152 | tf_op jit(solution)/shard_map/pallas_call | solution.py:424
  20.0 1.7 %collective-permute-start.9 = (s32[2,16,1024]{2,1,0:T(8,128)S(1)}, s32[2,16,1024]{2,1,0:T(8,128)S(1)}, u32[]{:S(2)}, u32[]{:S(2)}) collective-permute-start(s32[2,16,1024]{2,1,0:T(8,128)S(1)} %get-tuple-element.48.own), channel_id=1, source_target_pairs={{0,3},{1,2},{2,1},{3,0},{4,7},{5,6},{6,5},{7,4},{8,11},{9,10},{10,... | collective-permute-start | bytes 393224 | tf_op jit(solution)/shard_map/ppermute | solution.py:455
  21.8 1.0 %collective-permute-done.3.w2 = f32[2,16,1024]{2,1,0:T(8,128)S(1)} collective-permute-done((f32[2,16,1024]{2,1,0:T(8,128)S(1)}, f32[2,16,1024]{2,1,0:T(8,128)S(1)}, u32[]{:S(2)}, u32[]{:S(2)}) %collective-permute-start.3) | collective-permute-done | bytes 131104 | tf_op jit(solution)/shard_map/ppermute | solution.py:455
  22.8 1.9 %collective-permute-done.4.w3 = f32[2,16,1024]{2,1,0:T(8,128)S(1)} collective-permute-done((f32[2,16,1024]{2,1,0:T(8,128)S(1)}, f32[2,16,1024]{2,1,0:T(8,128)S(1)}, u32[]{:S(2)}, u32[]{:S(2)}) %collective-permute-start.4) | collective-permute-done | bytes 131104 | tf_op jit(solution)/shard_map/ppermute | solution.py:455
  24.7 8.4 %shard_map.78 = (f32[2,8,64,128]{3,2,1,0:T(8,128)S(1)}, f32[3,16,1024]{2,1,0:T(8,128)S(1)}, f32[3,16,1024]{2,1,0:T(8,128)S(1)}, f32[3,16,1024]{2,1,0:T(8,128)S(1)}, f32[3,16,1024]{2,1,0:T(8,128)S(1)}) custom-call(s32[2]{0:T(128)S(1)} %pad_add_fusion.1.lane_ref, f32[2,16,1024]{2,1,0:T(8,128)S(1)} %collective-permute-done.w0, ...), custom_call_target="tpu_custom_call" | custom-call | flops 10485760 | bytes 41943040 | tf_op jit(solution)/shard_map/pallas_call | solution.py:424
  33.2 0.7 collective-permute-start.10
  34.2 3.0 %collective-permute-start.12 = (f32[3,16,1024]{2,1,0:T(8,128)S(1)}, f32[3,16,1024]{2,1,0:T(8,128)S(1)}, u32[]{:S(2)}, u32[]{:S(2)}) collective-permute-start(f32[3,16,1024]{2,1,0:T(8,128)S(1)} %get-tuple-element.58), channel_id=1, source_target_pairs={{0,14},{1,15},{2,0},{3,1},{4,2},{5,3},{6,4},{7,5},{8,6},{9,7},{10,... | collective-permute-start | bytes 589832 | tf_op jit(solution)/shard_map/ppermute | solution.py:455
  37.3 1.0 %shard_map.79.cells = s32[2,8,64,128]{3,2,1,0:T(8,128)S(1)} custom-call(s32[2]{0:T(128)S(1)} %pad_add_fusion.1.lane_ref, s32[2,16,1024]{2,1,0:T(8,128)S(1)} %get-tuple-element.48.own, s32[2,16,1024]{2,1,0:T(8,128)S(1)} %collective-permute-done.7.two, s32[2,16,1024]{2,1,0:T(8,128)S(1)} %collective-permute-done.8.one, ...), custom_call_target="tpu_custom_call" | custom-call | flops 524288 | bytes 2097152 | tf_op jit(solution)/shard_map/pallas_call | solution.py:424
  38.2 7.9 %shard_map.80 = (f32[3,16,1024]{2,1,0:T(8,128)S(1)}, f32[3,16,1024]{2,1,0:T(8,128)S(1)}, f32[3,16,1024]{2,1,0:T(8,128)S(1)}, f32[3,16,1024]{2,1,0:T(8,128)S(1)}) custom-call(s32[2]{0:T(128)S(1)} %pad_add_fusion.1.lane_ref, f32[2,8,64,128]{3,2,1,0:T(8,128)S(1)} %get-tuple-element.42.wave, s32[2,8,64,128]{3,2,1,0:T(8,128)S(1)} %shard_map.79.cells, ...), custom_call_target="tpu_custom_call" | custom-call | flops 10485760 | bytes 41943040 | tf_op jit(solution)/shard_map/pallas_call | solution.py:424
  46.2 0.9 %collective-permute-done.13.n3 = f32[3,16,1024]{2,1,0:T(8,128)S(1)} collective-permute-done((f32[3,16,1024]{2,1,0:T(8,128)S(1)}, f32[3,16,1024]{2,1,0:T(8,128)S(1)}, u32[]{:S(2)}, u32[]{:S(2)}) %collective-permute-start.13) | collective-permute-done | bytes 196640 | tf_op jit(solution)/shard_map/ppermute | solution.py:455
  47.1 2.7 %collective-permute-start.14 = (f32[3,16,1024]{2,1,0:T(8,128)S(1)}, f32[3,16,1024]{2,1,0:T(8,128)S(1)}, u32[]{:S(2)}, u32[]{:S(2)}) collective-permute-start(f32[3,16,1024]{2,1,0:T(8,128)S(1)} %get-tuple-element.60), channel_id=1, source_target_pairs={{0,4},{1,5},{2,2},{3,3},{4,8},{5,9},{6,6},{7,7},{8,12},{9,13},{10,... | collective-permute-start | bytes 589832 | tf_op jit(solution)/shard_map/ppermute | solution.py:455
  49.9 0.5 collective-permute-start.16
  50.4 0.5 collective-permute-start.17
  50.9 7.7 %collective-permute-done.14.m0 = f32[3,16,1024]{2,1,0:T(8,128)S(1)} collective-permute-done((f32[3,16,1024]{2,1,0:T(8,128)S(1)}, f32[3,16,1024]{2,1,0:T(8,128)S(1)}, u32[]{:S(2)}, u32[]{:S(2)}) %collective-permute-start.14) | collective-permute-done | bytes 196640 | tf_op jit(solution)/shard_map/ppermute | solution.py:455
  58.5 2.5 %collective-permute-done.15.m1 = f32[3,16,1024]{2,1,0:T(8,128)S(1)} collective-permute-done((f32[3,16,1024]{2,1,0:T(8,128)S(1)}, f32[3,16,1024]{2,1,0:T(8,128)S(1)}, u32[]{:S(2)}, u32[]{:S(2)}) %collective-permute-start.15) | collective-permute-done | bytes 196640 | tf_op jit(solution)/shard_map/ppermute | solution.py:455
  61.0 2.0 %collective-permute-done.17.m3 = f32[3,16,1024]{2,1,0:T(8,128)S(1)} collective-permute-done((f32[3,16,1024]{2,1,0:T(8,128)S(1)}, f32[3,16,1024]{2,1,0:T(8,128)S(1)}, u32[]{:S(2)}, u32[]{:S(2)}) %collective-permute-start.17) | collective-permute-done | bytes 196640 | tf_op jit(solution)/shard_map/ppermute | solution.py:455
  63.1 0.7 %shard_map.81 = (f32[2,16,1024]{2,1,0:T(8,128)S(1)}, f32[8,128]{1,0:T(8,128)S(1)}) custom-call(s32[2]{0:T(128)S(1)} %pad_add_fusion.1.lane_ref, f32[3,16,1024]{2,1,0:T(8,128)S(1)} %collective-permute-done.14.m0, f32[3,16,1024]{2,1,0:T(8,128)S(1)} %collective-permute-done.15.m1, f32[3,16,1024]{2,1,0:T(8,128)S(1)} %collective-permute-done.16.m2, ...), custom_call_target="tpu_custom_call" | custom-call | flops 262144 | bytes 1048576 | tf_op jit(solution)/shard_map/pallas_call | solution.py:424
  63.8 0.6 collective-permute-start.18
  64.4 1.0 %collective-permute-start.19 = (f32[8,128]{1,0:T(8,128)S(1)}, f32[8,128]{1,0:T(8,128)S(1)}, u32[]{:S(2)}, u32[]{:S(2)}) collective-permute-start(f32[8,128]{1,0:T(8,128)S(1)} %get-tuple-element.70.s0), channel_id=1, source_target_pairs={{2,4},{3,5},{4,2},{5,3},{6,8},{7,9},{8,6},{9,7},{10,12},{11,13},{1... | collective-permute-start | bytes 12296 | tf_op jit(solution)/shard_map/ppermute | solution.py:455
  65.4 3.1 %collective-permute-start.20 = (f32[8,128]{1,0:T(8,128)S(1)}, f32[8,128]{1,0:T(8,128)S(1)}, u32[]{:S(2)}, u32[]{:S(2)}) collective-permute-start(f32[8,128]{1,0:T(8,128)S(1)} %get-tuple-element.70.s0), channel_id=1, source_target_pairs={{2,5},{3,4},{4,3},{5,2},{6,9},{7,8},{8,7},{9,6},{10,13},{11,12},{1... | collective-permute-start | bytes 12296 | tf_op jit(solution)/shard_map/ppermute | solution.py:455
  68.6 1.8 %shard_map.82 = (f32[4,2,16,1024]{3,2,1,0:T(8,128)}, f32[2,16,1024]{2,1,0:T(8,128)S(1)}) custom-call(s32[2]{0:T(128)S(1)} %pad_add_fusion.1.lane_ref, f32[3,16,1024]{2,1,0:T(8,128)S(1)} %collective-permute-done.14.m0, f32[3,16,1024]{2,1,0:T(8,128)S(1)} %collective-permute-done.15.m1, f32[3,16,1024]{2,1,0:T(8,128)S(1)} %collective-permute-done.16.m2, ...), custom_call_target="tpu_custom_call" | custom-call | flops 1048576 | bytes 4194304 | tf_op jit(solution)/shard_map/pallas_call | solution.py:424
  71.1 0.8 %shard_map.83 = f32[2,16,1024]{2,1,0:T(8,128)} custom-call(s32[1]{0:T(128)} %constant.67.clone.1.cells_ref, f32[2,16,1024]{2,1,0:T(8,128)S(1)} %get-tuple-element.69.raw, f32[8,128]{1,0:T(8,128)S(1)} %get-tuple-element.70.s0, f32[8,128]{1,0:T(8,128)S(1)} %collective-permute-done.18.s1, f32[8,128]{1,0:T(8,128)S(1)} %collective-permute-done.19.s2, ...), custom_call_target="tpu_custom_call" | custom-call | flops 131072 | bytes 524288 | tf_op jit(solution)/shard_map/pallas_call | solution.py:424
  (38 shorter events, 2.7 us)
Async XLA Ops:
  0.6 17.4 %copy-start = (f32[16,16,2,13]{1,2,3,0:T(2,128)S(1)}, f32[16,16,2,13]{1,2,3,0:T(2,128)}, u32[]{:S(2)}) copy-start(f32[16,16,2,13]{1,2,3,0:T(2,128)} %param.9) | copy-start | bytes 79876
  0.6 8.2 %collective-permute-start.2 = (s32[2,16,1024]{2,1,0:T(8,128)}, s32[2,16,1024]{2,1,0:T(8,128)S(1)}, u32[]{:S(2)}, u32[]{:S(2)}) collective-permute-start(s32[2,16,1024]{2,1,0:T(8,128)} %param.7), channel_id=1, source_target_pairs={{0,12},{1,13},{2,6},{3,7},{4,0},{5,1},{6,10},{7,11},{8,4},{9,5},{1... | collective-permute-start | bytes 393224 | tf_op jit(solution)/shard_map/ppermute | solution.py:455
  5.7 3.1 %copy-start.1 = (s32[2,16,1024]{2,1,0:T(8,128)S(1)}, s32[2,16,1024]{2,1,0:T(8,128)}, u32[]{:S(2)}) copy-start(s32[2,16,1024]{2,1,0:T(8,128)} %param.7) | copy-start | bytes 393220
  6.9 12.9 %collective-permute-start = (f32[2,16,1024]{2,1,0:T(8,128)S(1)}, f32[2,16,1024]{2,1,0:T(8,128)S(1)}, u32[]{:S(2)}, u32[]{:S(2)}) collective-permute-start(f32[2,16,1024]{2,1,0:T(8,128)S(1)} %get-tuple-element.74), channel_id=1, source_target_pairs={{0,0},{1,1},{2,6},{3,7},{4,4},{5,5},{6,10},{7,11},{8,8},{9,9},{10,... | collective-permute-start | bytes 393224 | tf_op jit(solution)/shard_map/ppermute | solution.py:455
  7.6 12.4 %collective-permute-start.1 = (f32[2,16,1024]{2,1,0:T(8,128)S(1)}, f32[2,16,1024]{2,1,0:T(8,128)S(1)}, u32[]{:S(2)}, u32[]{:S(2)}) collective-permute-start(f32[2,16,1024]{2,1,0:T(8,128)S(1)} %get-tuple-element.73), channel_id=1, source_target_pairs={{0,1},{1,0},{2,7},{3,6},{4,5},{5,4},{6,11},{7,10},{8,9},{9,8},{10,... | collective-permute-start | bytes 393224 | tf_op jit(solution)/shard_map/ppermute | solution.py:455
  8.8 7.6 %collective-permute-start.5 = (s32[2,16,1024]{2,1,0:T(8,128)S(1)}, s32[2,16,1024]{2,1,0:T(8,128)S(1)}, u32[]{:S(2)}, u32[]{:S(2)}) collective-permute-start(s32[2,16,1024]{2,1,0:T(8,128)S(1)} %get-tuple-element.39.own), channel_id=1, source_target_pairs={{0,2},{1,3},{2,0},{3,1},{4,6},{5,7},{6,4},{7,5},{8,10},{9,11},{10,... | collective-permute-start | bytes 393224 | tf_op jit(solution)/shard_map/ppermute | solution.py:455
  13.7 2.1 %copy-start.3 = (f32[16]{0:T(128)S(1)}, f32[16]{0:T(128)}, u32[]{:S(2)}) copy-start(f32[16]{0:T(128)} %param.10) | copy-start | bytes 196
  13.7 9.1 %collective-permute-start.3 = (f32[2,16,1024]{2,1,0:T(8,128)S(1)}, f32[2,16,1024]{2,1,0:T(8,128)S(1)}, u32[]{:S(2)}, u32[]{:S(2)}) collective-permute-start(f32[2,16,1024]{2,1,0:T(8,128)S(1)} %get-tuple-element.37), channel_id=1, source_target_pairs={{0,2},{1,3},{2,4},{3,5},{4,6},{5,7},{6,8},{7,9},{8,10},{9,11},{10,... | collective-permute-start | bytes 393224 | tf_op jit(solution)/shard_map/ppermute | solution.py:455
  13.8 10.9 %collective-permute-start.4 = (f32[2,16,1024]{2,1,0:T(8,128)S(1)}, f32[2,16,1024]{2,1,0:T(8,128)S(1)}, u32[]{:S(2)}, u32[]{:S(2)}) collective-permute-start(f32[2,16,1024]{2,1,0:T(8,128)S(1)} %get-tuple-element.38), channel_id=1, source_target_pairs={{0,3},{1,2},{2,5},{3,4},{4,7},{5,6},{6,9},{7,8},{8,11},{9,10},{10,... | collective-permute-start | bytes 393224 | tf_op jit(solution)/shard_map/ppermute | solution.py:455
  16.5 0.9 %copy-start.2 = (f32[16]{0:T(128)S(1)}, f32[16]{0:T(128)}, u32[]{:S(2)}) copy-start(f32[16]{0:T(128)} %param.11) | copy-start | bytes 196
  16.5 2.0 %collective-permute-start.6 = (s32[2,2,16,1024]{3,2,1,0:T(8,128)S(1)}, s32[2,2,16,1024]{3,2,1,0:T(8,128)S(1)}, u32[]{:S(2)}, u32[]{:S(2)}) collective-permute-start(s32[2,2,16,1024]{3,2,1,0:T(8,128)S(1)} %pad_add_fusion), channel_id=1, source_target_pairs={{0,1},{1,0},{2,3},{3,2},{4,5},{5,4},{6,7},{7,6},{8,9},{9,8},{10,11... | collective-permute-start | bytes 786440 | tf_op jit(solution)/shard_map/ppermute | solution.py:455
  19.5 13.7 %collective-permute-start.7 = (s32[2,16,1024]{2,1,0:T(8,128)S(1)}, s32[2,16,1024]{2,1,0:T(8,128)S(1)}, u32[]{:S(2)}, u32[]{:S(2)}) collective-permute-start(s32[2,16,1024]{2,1,0:T(8,128)S(1)} %get-tuple-element.48.own), channel_id=1, source_target_pairs={{0,2},{1,3},{2,0},{3,1},{4,6},{5,7},{6,4},{7,5},{8,10},{9,11},{10,... | collective-permute-start | bytes 393224 | tf_op jit(solution)/shard_map/ppermute | solution.py:455
  19.8 13.3 %collective-permute-start.8 = (s32[2,16,1024]{2,1,0:T(8,128)S(1)}, s32[2,16,1024]{2,1,0:T(8,128)S(1)}, u32[]{:S(2)}, u32[]{:S(2)}) collective-permute-start(s32[2,16,1024]{2,1,0:T(8,128)S(1)} %get-tuple-element.48.own), channel_id=1, source_target_pairs={{0,1},{1,0},{2,3},{3,2},{4,5},{5,4},{6,7},{7,6},{8,9},{9,8},{10,11... | collective-permute-start | bytes 393224 | tf_op jit(solution)/shard_map/ppermute | solution.py:455
  20.0 13.2 %collective-permute-start.9 = (s32[2,16,1024]{2,1,0:T(8,128)S(1)}, s32[2,16,1024]{2,1,0:T(8,128)S(1)}, u32[]{:S(2)}, u32[]{:S(2)}) collective-permute-start(s32[2,16,1024]{2,1,0:T(8,128)S(1)} %get-tuple-element.48.own), channel_id=1, source_target_pairs={{0,3},{1,2},{2,1},{3,0},{4,7},{5,6},{6,5},{7,4},{8,11},{9,10},{10,... | collective-permute-start | bytes 393224 | tf_op jit(solution)/shard_map/ppermute | solution.py:455
  33.2 12.9 %collective-permute-start.10 = (f32[3,16,1024]{2,1,0:T(8,128)S(1)}, f32[3,16,1024]{2,1,0:T(8,128)S(1)}, u32[]{:S(2)}, u32[]{:S(2)}) collective-permute-start(f32[3,16,1024]{2,1,0:T(8,128)S(1)} %get-tuple-element.56), channel_id=1, source_target_pairs={{0,0},{1,1},{2,14},{3,15},{4,4},{5,5},{6,2},{7,3},{8,8},{9,9},{10,... | collective-permute-start | bytes 589832 | tf_op jit(solution)/shard_map/ppermute | solution.py:455
  33.9 12.3 %collective-permute-start.11 = (f32[3,16,1024]{2,1,0:T(8,128)S(1)}, f32[3,16,1024]{2,1,0:T(8,128)S(1)}, u32[]{:S(2)}, u32[]{:S(2)}) collective-permute-start(f32[3,16,1024]{2,1,0:T(8,128)S(1)} %get-tuple-element.57), channel_id=1, source_target_pairs={{0,1},{1,0},{2,15},{3,14},{4,5},{5,4},{6,3},{7,2},{8,9},{9,8},{10,... | collective-permute-start | bytes 589832 | tf_op jit(solution)/shard_map/ppermute | solution.py:455
  34.2 11.9 %collective-permute-start.12 = (f32[3,16,1024]{2,1,0:T(8,128)S(1)}, f32[3,16,1024]{2,1,0:T(8,128)S(1)}, u32[]{:S(2)}, u32[]{:S(2)}) collective-permute-start(f32[3,16,1024]{2,1,0:T(8,128)S(1)} %get-tuple-element.58), channel_id=1, source_target_pairs={{0,14},{1,15},{2,0},{3,1},{4,2},{5,3},{6,4},{7,5},{8,6},{9,7},{10,... | collective-permute-start | bytes 589832 | tf_op jit(solution)/shard_map/ppermute | solution.py:455
  37.3 9.9 %collective-permute-start.13 = (f32[3,16,1024]{2,1,0:T(8,128)S(1)}, f32[3,16,1024]{2,1,0:T(8,128)S(1)}, u32[]{:S(2)}, u32[]{:S(2)}) collective-permute-start(f32[3,16,1024]{2,1,0:T(8,128)S(1)} %get-tuple-element.59), channel_id=1, source_target_pairs={{0,15},{1,14},{2,1},{3,0},{4,3},{5,2},{6,5},{7,4},{8,7},{9,6},{10,... | collective-permute-start | bytes 589832 | tf_op jit(solution)/shard_map/ppermute | solution.py:455
  47.1 11.4 %collective-permute-start.14 = (f32[3,16,1024]{2,1,0:T(8,128)S(1)}, f32[3,16,1024]{2,1,0:T(8,128)S(1)}, u32[]{:S(2)}, u32[]{:S(2)}) collective-permute-start(f32[3,16,1024]{2,1,0:T(8,128)S(1)} %get-tuple-element.60), channel_id=1, source_target_pairs={{0,4},{1,5},{2,2},{3,3},{4,8},{5,9},{6,6},{7,7},{8,12},{9,13},{10,... | collective-permute-start | bytes 589832 | tf_op jit(solution)/shard_map/ppermute | solution.py:455
  49.8 11.2 %collective-permute-start.15 = (f32[3,16,1024]{2,1,0:T(8,128)S(1)}, f32[3,16,1024]{2,1,0:T(8,128)S(1)}, u32[]{:S(2)}, u32[]{:S(2)}) collective-permute-start(f32[3,16,1024]{2,1,0:T(8,128)S(1)} %get-tuple-element.61), channel_id=1, source_target_pairs={{0,5},{1,4},{2,3},{3,2},{4,9},{5,8},{6,7},{7,6},{8,13},{9,12},{10,... | collective-permute-start | bytes 589832 | tf_op jit(solution)/shard_map/ppermute | solution.py:455
  49.9 11.2 %collective-permute-start.16 = (f32[3,16,1024]{2,1,0:T(8,128)S(1)}, f32[3,16,1024]{2,1,0:T(8,128)S(1)}, u32[]{:S(2)}, u32[]{:S(2)}) collective-permute-start(f32[3,16,1024]{2,1,0:T(8,128)S(1)} %get-tuple-element.62), channel_id=1, source_target_pairs={{0,2},{1,3},{2,4},{3,5},{4,6},{5,7},{6,8},{7,9},{8,10},{9,11},{10,... | collective-permute-start | bytes 589832 | tf_op jit(solution)/shard_map/ppermute | solution.py:455
  50.4 12.6 %collective-permute-start.17 = (f32[3,16,1024]{2,1,0:T(8,128)S(1)}, f32[3,16,1024]{2,1,0:T(8,128)S(1)}, u32[]{:S(2)}, u32[]{:S(2)}) collective-permute-start(f32[3,16,1024]{2,1,0:T(8,128)S(1)} %get-tuple-element.63), channel_id=1, source_target_pairs={{0,3},{1,2},{2,5},{3,4},{4,7},{5,6},{6,9},{7,8},{8,11},{9,10},{10,... | collective-permute-start | bytes 589832 | tf_op jit(solution)/shard_map/ppermute | solution.py:455
  63.8 6.6 %collective-permute-start.18 = (f32[8,128]{1,0:T(8,128)S(1)}, f32[8,128]{1,0:T(8,128)S(1)}, u32[]{:S(2)}, u32[]{:S(2)}) collective-permute-start(f32[8,128]{1,0:T(8,128)S(1)} %get-tuple-element.70.s0), channel_id=1, source_target_pairs={{2,3},{3,2},{4,5},{5,4},{6,7},{7,6},{8,9},{9,8},{10,11},{11,10},{1... | collective-permute-start | bytes 12296 | tf_op jit(solution)/shard_map/ppermute | solution.py:455
  64.4 6.3 %collective-permute-start.19 = (f32[8,128]{1,0:T(8,128)S(1)}, f32[8,128]{1,0:T(8,128)S(1)}, u32[]{:S(2)}, u32[]{:S(2)}) collective-permute-start(f32[8,128]{1,0:T(8,128)S(1)} %get-tuple-element.70.s0), channel_id=1, source_target_pairs={{2,4},{3,5},{4,2},{5,3},{6,8},{7,9},{8,6},{9,7},{10,12},{11,13},{1... | collective-permute-start | bytes 12296 | tf_op jit(solution)/shard_map/ppermute | solution.py:455
  65.4 5.7 %collective-permute-start.20 = (f32[8,128]{1,0:T(8,128)S(1)}, f32[8,128]{1,0:T(8,128)S(1)}, u32[]{:S(2)}, u32[]{:S(2)}) collective-permute-start(f32[8,128]{1,0:T(8,128)S(1)} %get-tuple-element.70.s0), channel_id=1, source_target_pairs={{2,5},{3,4},{4,3},{5,2},{6,9},{7,8},{8,7},{9,6},{10,13},{11,12},{1... | collective-permute-start | bytes 12296 | tf_op jit(solution)/shard_map/ppermute | solution.py:455
